TPU v7x, 32 devices: a whole 2x2x4 slice. The times are simulated.
32 devices in a mesh: row: 8 (over z, x), col: 4 (over y, core).
Axes of the slice: x: 2, y: 2, z: 4, core: 2. Of those that a mesh axis runs over, the one named last changes fastest.
Arguments:
- features: bfloat16 [48, 512, 512], P(None, 'row', 'col'), may hold values from -6 to 6
- w_dilated: bfloat16 [2, 3, 3, 48, 48], replicated, may hold values from -0.3125 to 0.3125
- w_pointwise: bfloat16 [2, 48, 48], replicated, may hold values from -0.875 to 0.875
- norm_gain: float32 [2, 2, 48], replicated, may hold values from 0.25 to 1.75
- norm_bias: float32 [2, 2, 48], replicated, may hold values from -0.5 to 0.5
Outputs:
- refined: bfloat16 [48, 512, 512], P(None, 'row', 'col')
All inputs are finite; a program needn't handle non-finite values.
Results may differ from a plain program's by a relative error of at most 0.0065.
Values may be sent and summed in bfloat16 or wider, within the bound.
A program may use at most 64 MiB of HBM per device.

v0:
```python
import jax
import jax.numpy as jnp
from jax import lax
from jax.sharding import PartitionSpec as P

FIRST_DILATION = 8
SECOND_DILATION = 16


def padded(value, sides, width):
    for axis, dim in sides:
        size, length = (lax.axis_size(axis), value.shape[dim])
        up = [(i, (i + 1) % size) for i in range(size - 1)]
        down = [(j, i) for i, j in up]
        last = lax.slice_in_dim(value, length - width, length, axis=dim)
        initial = lax.slice_in_dim(value, 0, width, axis=dim)
        before = lax.ppermute(last, axis, up)
        after = lax.ppermute(initial, axis, down)
        value = jnp.concatenate([before, value, after], axis=dim)
    return value


def dilated_terms(
    extended_input, current_state, kernel, gain_pair, bias_pair, pointwise, dilation_rate
):
    active = jnp.maximum(extended_input, jnp.zeros((), extended_input.dtype))
    spread = lax.conv_general_dilated(
        active[None],
        kernel,
        (1, 1),
        "VALID",
        rhs_dilation=(dilation_rate, dilation_rate),
        preferred_element_type=jnp.float32,
    )[0]
    hidden = jnp.maximum(
        spread * gain_pair[0][:, None, None] + bias_pair[0][:, None, None], 0.0
    ).astype(jnp.bfloat16)
    branch = jnp.einsum("oc,chw->ohw", pointwise, hidden, preferred_element_type=jnp.float32)
    summed = (
        current_state.astype(jnp.float32)
        + branch * gain_pair[1][:, None, None]
        + bias_pair[1][:, None, None]
    )
    return summed.astype(jnp.bfloat16)


def mirror_tile(output_map):
    n_row = lax.axis_size("row")
    n_col = lax.axis_size("col")
    channel_count, tile_rows, tile_cols = output_map.shape
    sub_rows = tile_rows // n_col
    ratio = n_row // n_col
    first_leg = lax.all_to_all(output_map, "col", split_axis=1, concat_axis=2, tiled=True)
    count = first_leg.shape[0]
    moved = lax.all_to_all(
        lax.all_to_all(first_leg, "row", split_axis=2, concat_axis=1, tiled=True),
        "col",
        split_axis=1,
        concat_axis=1,
        tiled=True,
    )
    grouped = moved.reshape(count, n_col, ratio, sub_rows, tile_rows)
    return jnp.transpose(grouped, (0, 4, 2, 1, 3)).reshape(count, tile_rows, tile_cols)


def body(features, w_dilated, w_pointwise, norm_gain, norm_bias):
    current_state = features
    for layer_index in range(2):
        if layer_index == 0:
            dilation_rate = FIRST_DILATION
            extended_input = padded(current_state, (("row", 1), ("col", 2)), FIRST_DILATION)
        else:
            dilation_rate = SECOND_DILATION
            extended_input = padded(current_state, (("row", 1), ("col", 2)), SECOND_DILATION)
        kernel = jnp.transpose(w_dilated[layer_index], (2, 3, 0, 1))
        output_map = dilated_terms(
            extended_input,
            current_state,
            kernel,
            norm_gain[layer_index],
            norm_bias[layer_index],
            w_pointwise[layer_index],
            dilation_rate,
        )
        if layer_index == 0:
            mirrored = mirror_tile(output_map)
        else:
            mirrored = mirror_tile(output_map)
        output_map, mirrored = lax.optimization_barrier((output_map, mirrored))
        current_state = (
            (output_map.astype(jnp.float32) + mirrored.astype(jnp.float32)) * 0.5
        ).astype(jnp.bfloat16)
    return current_state


def solution(mesh):
    in_specs = (P(None, "row", "col"), P(), P(), P(), P())
    out_specs = P(None, "row", "col")
    return jax.shard_map(body, mesh=mesh, in_specs=in_specs, out_specs=out_specs, check_vma=False)
```

profile of v0, /device:TPU:0, one launch (start us, length us, event | category | flops | bytes accessed | tf_op | source)
XLA Modules:
  0.0 292.0 jit_solution(3096498368182103932)
XLA Ops:
  1.0 4.8 %collective-permute-start = (bf16[48,8,128]{2,1,0:T(8,128)(2,1)S(1)}, bf16[48,8,128]{2,1,0:T(8,128)(2,1)S(1)}, u32[]{:S(2)}, u32[]{:S(2)}) collective-permute-start(bf16[48,8,128]{2,1,0:T(8,128)(2,1)S(1)} %get-tuple-element.19), channel_id=1, source_target_pairs={{0,4},{4,8},{8,12},{12,16},{16,20},{20,24},{24,28},{1,5},{5,9},{9,... | collective-permute-start | bytes 294920 | tf_op jit(solution)/shard_map/ppermute | solution.py:17
  8.0 1.9 copy.146
  9.9 1.5 copy.144
  13.3 1.7 copy.145
  15.0 3.0 %pad_maximum_fusion = bf16[48,80,128]{1,0,2:T(8,128)(2,1)S(1)} fusion(bf16[48,8,128]{1,0,2:T(8,128)(2,1)S(1)} %copy.147, bf16[48,64,128]{1,0,2:T(8,128)(2,1)S(1)} %copy.146, bf16[48,8,128]{1,0,2:T(8,128)(2,1)} %copy.145), kind=kLoop, calls=%fused_computation.20 | loop fusion | flops 2949120 | bytes 1966080 | tf_op jit(solution)/shard_map/concatenate | solution.py:19
  19.3 1.6 collective-permute-start.3
  22.4 1.9 collective-permute-done.3
  24.3 1.7 maximum_maximum_fusion.1
  26.0 3.6 %copy.149 = bf16[48,80,1,8,18]{0,3,4,1,2:T(8,128)(2,1)S(1)} copy(bf16[48,80,1,8,18]{1,0,4,3,2:T(8,128)(2,1)} %bitcast.105) | data formatting | bytes 2211840 | tf_op jit(solution)/shard_map/conv_general_dilated | solution.py:27
  30.6 7.9 %maximum_convert_fusion = bf16[64,8,18,48]{3,1,2,0:T(8,128)(2,1)} fusion(f32[48]{0:T(128)S(1)} %get-tuple-element.27, f32[48]{0:T(128)S(1)} %get-tuple-element.30, pred[8,18]{0,1:T(8,128)(4,1)S(1)} %copy-done.6, bf16[48,80,1,7,16]{0,3,4,1,2:T(8,128)(2,1)S(1)} %slice.104, bf16[48,80,1,8,18]{0,3,4,1,2:T(8,128)(2,1)S(1)} %copy.149, ...), kind=kOutput, calls=%fused_computation.8 | convolution fusion | flops 390684672 | bytes 6569984 | tf_op jit(solution)/shard_map/conv_general_dilated | solution.py:27
  38.5 3.6 %copy.150 = bf16[64,8,18,48]{0,3,2,1:T(8,128)(2,1)S(1)} copy(bf16[64,8,18,48]{3,1,2,0:T(8,128)(2,1)} %maximum_convert_fusion) | data formatting | bytes 1769472 | tf_op jit(solution)/shard_map/convert_element_type | solution.py:37
  42.2 1.9 copy.186
  44.1 1.5 fusion.16
  45.6 2.2 copy.152
  47.8 3.0 %fusion.11 = bf16[48,64,128]{1,2,0:T(8,128)(2,1)S(1)} fusion(f32[64,128,48]{0,1,2:T(8,128)} %copy.152, bf16[48,64,128]{1,2,0:T(8,128)(2,1)} %copy.144, f32[48]{0:T(128)S(1)} %get-tuple-element.26, f32[48]{0:T(128)S(1)} %get-tuple-element.31), kind=kLoop, calls=%fused_computation.14 | loop fusion | flops 1966080 | bytes 3146112 | tf_op jit(solution)/shard_map/convert_element_type | solution.py:44
  51.6 16.5 %all_to_all.82 = bf16[48,64,128]{2,0,1:T(8,128)(2,1)S(1)} all-to-all(bf16[48,64,128]{2,0,1:T(8,128)(2,1)S(1)} %copy.153), channel_id=1, replica_groups=mesh['row'=8,'col'=4] {'col'}, dimensions={1} | all-to-all | bytes 1572864 | tf_op jit(solution)/shard_map/all_to_all | solution.py:53
  68.1 2.5 copy.179
  70.6 5.2 %reshape.140 = bf16[8,2,24576]{2,1,0:T(2,128)(2,1)S(1)} reshape(bf16[512,16,48]{2,1,0:T(8,128)(2,1)} %bitcast.103) | data formatting | bytes 1572864
  75.8 25.6 %all_to_all.83 = bf16[8,2,24576]{2,1,0:T(2,128)(2,1)S(1)} all-to-all(bf16[8,2,24576]{2,1,0:T(2,128)(2,1)S(1)} %reshape.140), channel_id=1, replica_groups=mesh['row'=8,'col'=4] {'row'}, dimensions={0} | all-to-all | bytes 1572864 | tf_op jit(solution)/shard_map/all_to_all | solution.py:56
  101.4 3.1 %reshape.141 = bf16[512,16,48]{2,1,0:T(8,128)(2,1)} reshape(bf16[8,2,24576]{2,1,0:T(2,128)(2,1)S(1)} %all_to_all.83) | data formatting | bytes 1572864
  104.5 4.2 %copy.157 = bf16[48,16,8,64]{3,1,2,0:T(8,128)(2,1)S(1)} copy(bf16[48,16,8,64]{0,1,3,2:T(8,128)(2,1)} %bitcast.101) | data formatting | bytes 1572864 | tf_op jit(solution)/shard_map/all_to_all | solution.py:56
  108.7 2.2 copy.192
  110.9 3.0 %reshape.142 = bf16[4,2,49152]{2,1,0:T(2,128)(2,1)S(1)} reshape(bf16[128,48,64]{2,1,0:T(8,128)(2,1)} %bitcast.108) | data formatting | bytes 1572864
  114.0 14.8 %all_to_all.84 = bf16[4,2,49152]{2,1,0:T(2,128)(2,1)} all-to-all(bf16[4,2,49152]{2,1,0:T(2,128)(2,1)S(1)} %reshape.142), channel_id=1, replica_groups=mesh['row'=8,'col'=4] {'col'}, dimensions={0} | all-to-all | bytes 1572864 | tf_op jit(solution)/shard_map/all_to_all | solution.py:55
  128.7 2.8 reshape.143
  132.5 1.9 fusion.31
  134.4 1.6 copy.161
  136.1 3.4 %collective-permute-start.4 = (bf16[48,16,128]{2,1,0:T(8,128)(2,1)S(1)}, bf16[48,16,128]{2,1,0:T(8,128)(2,1)S(1)}, u32[]{:S(2)}, u32[]{:S(2)}) collective-permute-start(bf16[48,16,128]{2,1,0:T(8,128)(2,1)S(1)} %copy.161), channel_id=1, source_target_pairs={{0,4},{4,8},{8,12},{12,16},{16,20},{20,24},{24,28},{1,5},{5,9},{9,... | collective-permute-start | bytes 589832 | tf_op jit(solution)/shard_map/ppermute | solution.py:17
  144.0 4.9 %collective-permute-done.5 = bf16[48,16,128]{2,1,0:T(8,128)(2,1)} collective-permute-done((bf16[48,16,128]{2,1,0:T(8,128)(2,1)}, bf16[48,16,128]{2,1,0:T(8,128)(2,1)}, u32[]{:S(2)}, u32[]{:S(2)}) %collective-permute-start.5) | collective-permute-done | bytes 196640 | tf_op jit(solution)/shard_map/ppermute | solution.py:18
  148.9 2.4 copy.164
  151.3 3.0 %pad_maximum_fusion.1 = bf16[48,96,128]{1,2,0:T(8,128)(2,1)S(1)} fusion(bf16[48,16,128]{1,2,0:T(8,128)(2,1)} %copy.164, bf16[48,64,128]{1,2,0:T(8,128)(2,1)S(1)} %multiply_convert_fusion.1, bf16[48,16,128]{1,2,0:T(8,128)(2,1)S(1)} %copy.163), kind=kLoop, calls=%fused_computation.21 | loop fusion | flops 3538944 | bytes 2359296 | tf_op jit(solution)/shard_map/concatenate | solution.py:19
  155.6 1.5 collective-permute-start.7
  157.1 1.4 fusion.35
  160.5 11.8 %copy.165 = bf16[1,48,96,160]{1,0,3,2:T(2,128)(2,1)} copy(bf16[1,48,96,160]{2,3,1,0:T(8,128)(2,1)S(1)} %maximum_maximum_fusion) | data formatting | bytes 2949120 | tf_op jit(solution)/shard_map/max | solution.py:26
  172.3 26.8 %fusion.22 = f32[1,48,64,128]{1,0,3,2:T(1,128)} fusion(bf16[1,48,96,160]{1,0,3,2:T(2,128)(2,1)} %copy.165, bf16[2,3,3,48,48]{4,3,2,1,0:T(8,128)(2,1)} %param.6), kind=kOutput, calls=%fused_computation.31 | convolution fusion | flops 339738624 | bytes 9547776 | tf_op jit(solution)/shard_map/conv_general_dilated | solution.py:27
  199.2 5.3 %copy.166 = f32[1,48,64,128]{3,2,1,0:T(8,128)S(1)} copy(f32[1,48,64,128]{1,0,3,2:T(1,128)} %fusion.22) | data formatting | bytes 3145728 | tf_op jit(solution)/shard_map/conv_general_dilated | solution.py:27
  206.0 2.2 copy.168
  208.2 2.5 fusion.9
  211.7 16.9 %all_to_all.85 = bf16[48,64,128]{2,0,1:T(8,128)(2,1)S(1)} all-to-all(bf16[48,64,128]{2,0,1:T(8,128)(2,1)S(1)} %copy.169), channel_id=1, replica_groups=mesh['row'=8,'col'=4] {'col'}, dimensions={1} | all-to-all | bytes 1572864 | tf_op jit(solution)/shard_map/all_to_all | solution.py:53
  228.6 2.5 copy.182
  231.1 5.2 %reshape.144 = bf16[8,2,24576]{2,1,0:T(2,128)(2,1)S(1)} reshape(bf16[512,16,48]{2,1,0:T(8,128)(2,1)} %bitcast.104) | data formatting | bytes 1572864
  236.3 22.9 %all_to_all.86 = bf16[8,2,24576]{2,1,0:T(2,128)(2,1)S(1)} all-to-all(bf16[8,2,24576]{2,1,0:T(2,128)(2,1)S(1)} %reshape.144), channel_id=1, replica_groups=mesh['row'=8,'col'=4] {'row'}, dimensions={0} | all-to-all | bytes 1572864 | tf_op jit(solution)/shard_map/all_to_all | solution.py:56
  259.2 3.1 %reshape.145 = bf16[512,16,48]{2,1,0:T(8,128)(2,1)} reshape(bf16[8,2,24576]{2,1,0:T(2,128)(2,1)S(1)} %all_to_all.86) | data formatting | bytes 1572864
  262.3 4.2 %copy.173 = bf16[48,16,8,64]{3,1,2,0:T(8,128)(2,1)S(1)} copy(bf16[48,16,8,64]{0,1,3,2:T(8,128)(2,1)} %bitcast.102) | data formatting | bytes 1572864 | tf_op jit(solution)/shard_map/all_to_all | solution.py:56
  266.5 2.2 copy.191
  268.7 3.0 %reshape.146 = bf16[4,2,49152]{2,1,0:T(2,128)(2,1)S(1)} reshape(bf16[128,48,64]{2,1,0:T(8,128)(2,1)} %bitcast.111) | data formatting | bytes 1572864
  271.8 14.8 %all_to_all.87 = bf16[4,2,49152]{2,1,0:T(2,128)(2,1)} all-to-all(bf16[4,2,49152]{2,1,0:T(2,128)(2,1)S(1)} %reshape.146), channel_id=1, replica_groups=mesh['row'=8,'col'=4] {'col'}, dimensions={0} | all-to-all | bytes 1572864 | tf_op jit(solution)/shard_map/all_to_all | solution.py:55
  286.6 2.8 reshape.147
  (44 shorter events, 23.3 us)
Async XLA Ops:
  0.0 9.9 %copy-start.2 = (bf16[48,64,128]{2,1,0:T(8,128)(2,1)S(1)}, bf16[48,64,128]{2,1,0:T(8,128)(2,1)}, u32[]{:S(2)}) copy-start(bf16[48,64,128]{2,1,0:T(8,128)(2,1)} %param.5) | copy-start | bytes 2359300
  1.0 12.3 %collective-permute-start = (bf16[48,8,128]{2,1,0:T(8,128)(2,1)S(1)}, bf16[48,8,128]{2,1,0:T(8,128)(2,1)S(1)}, u32[]{:S(2)}, u32[]{:S(2)}) collective-permute-start(bf16[48,8,128]{2,1,0:T(8,128)(2,1)S(1)} %get-tuple-element.19), channel_id=1, source_target_pairs={{0,4},{4,8},{8,12},{12,16},{16,20},{20,24},{24,28},{1,5},{5,9},{9,... | collective-permute-start | bytes 294920 | tf_op jit(solution)/shard_map/ppermute | solution.py:17
  5.9 6.5 %collective-permute-start.1 = (bf16[48,8,128]{2,1,0:T(8,128)(2,1)S(1)}, bf16[48,8,128]{2,1,0:T(8,128)(2,1)S(1)}, u32[]{:S(2)}, u32[]{:S(2)}) collective-permute-start(bf16[48,8,128]{2,1,0:T(8,128)(2,1)S(1)} %get-tuple-element.20), channel_id=1, source_target_pairs={{4,0},{8,4},{12,8},{16,12},{20,16},{24,20},{28,24},{5,1},{9,5},{13... | collective-permute-start | bytes 294920 | tf_op jit(solution)/shard_map/ppermute | solution.py:18
  15.0 5.9 %copy-start = (bf16[48,8,128]{1,0,2:T(8,128)(2,1)S(1)}, bf16[48,8,128]{1,0,2:T(8,128)(2,1)}, u32[]{:S(2)}) copy-start(bf16[48,8,128]{1,0,2:T(8,128)(2,1)} %copy.145) | copy-start | bytes 294916
  18.0 4.3 %collective-permute-start.2 = (bf16[48,80,8]{1,0,2:T(8,128)(2,1)S(1)}, bf16[48,80,8]{1,0,2:T(8,128)(2,1)S(1)}, u32[]{:S(2)}, u32[]{:S(2)}) collective-permute-start(bf16[48,80,8]{1,0,2:T(8,128)(2,1)S(1)} %get-tuple-element.17), channel_id=1, source_target_pairs={{0,1},{1,2},{2,3},{4,5},{5,6},{6,7},{8,9},{9,10},{10,11},{12,13},{... | collective-permute-start | bytes 184328 | tf_op jit(solution)/shard_map/ppermute | solution.py:17
  19.3 4.9 %collective-permute-start.3 = (bf16[48,80,8]{1,0,2:T(8,128)(2,1)S(1)}, bf16[48,80,8]{1,0,2:T(8,128)(2,1)S(1)}, u32[]{:S(2)}, u32[]{:S(2)}) collective-permute-start(bf16[48,80,8]{1,0,2:T(8,128)(2,1)S(1)} %get-tuple-element.18), channel_id=1, source_target_pairs={{1,0},{2,1},{3,2},{5,4},{6,5},{7,6},{9,8},{10,9},{11,10},{13,12},{... | collective-permute-start | bytes 184328 | tf_op jit(solution)/shard_map/ppermute | solution.py:18
  29.6 0.9 copy-start.5
  29.6 0.9 copy-start.6
  42.2 1.9 copy-start.3
  136.1 7.1 %collective-permute-start.4 = (bf16[48,16,128]{2,1,0:T(8,128)(2,1)S(1)}, bf16[48,16,128]{2,1,0:T(8,128)(2,1)S(1)}, u32[]{:S(2)}, u32[]{:S(2)}) collective-permute-start(bf16[48,16,128]{2,1,0:T(8,128)(2,1)S(1)} %copy.161), channel_id=1, source_target_pairs={{0,4},{4,8},{8,12},{12,16},{16,20},{20,24},{24,28},{1,5},{5,9},{9,... | collective-permute-start | bytes 589832 | tf_op jit(solution)/shard_map/ppermute | solution.py:17
  140.7 8.2 %collective-permute-start.5 = (bf16[48,16,128]{2,1,0:T(8,128)(2,1)}, bf16[48,16,128]{2,1,0:T(8,128)(2,1)}, u32[]{:S(2)}, u32[]{:S(2)}) collective-permute-start(bf16[48,16,128]{2,1,0:T(8,128)(2,1)} %copy.162), channel_id=1, source_target_pairs={{4,0},{8,4},{12,8},{16,12},{20,16},{24,20},{28,24},{5,1},{9,5},{13... | collective-permute-start | bytes 589832 | tf_op jit(solution)/shard_map/ppermute | solution.py:18
  151.3 5.8 %copy-start.1 = (bf16[48,16,128]{1,2,0:T(8,128)(2,1)S(1)}, bf16[48,16,128]{1,2,0:T(8,128)(2,1)}, u32[]{:S(2)}) copy-start(bf16[48,16,128]{1,2,0:T(8,128)(2,1)} %copy.164) | copy-start | bytes 589828
  154.3 4.2 %collective-permute-start.6 = (bf16[48,96,16]{1,2,0:T(8,128)(2,1)S(1)}, bf16[48,96,16]{1,2,0:T(8,128)(2,1)S(1)}, u32[]{:S(2)}, u32[]{:S(2)}) collective-permute-start(bf16[48,96,16]{1,2,0:T(8,128)(2,1)S(1)} %get-tuple-element.13), channel_id=1, source_target_pairs={{0,1},{1,2},{2,3},{4,5},{5,6},{6,7},{8,9},{9,10},{10,11},{12,13},{... | collective-permute-start | bytes 442376 | tf_op jit(solution)/shard_map/ppermute | solution.py:17
  155.6 4.3 %collective-permute-start.7 = (bf16[48,96,16]{1,2,0:T(8,128)(2,1)S(1)}, bf16[48,96,16]{1,2,0:T(8,128)(2,1)S(1)}, u32[]{:S(2)}, u32[]{:S(2)}) collective-permute-start(bf16[48,96,16]{1,2,0:T(8,128)(2,1)S(1)} %get-tuple-element.14), channel_id=1, source_target_pairs={{1,0},{2,1},{3,2},{5,4},{6,5},{7,6},{9,8},{10,9},{11,10},{13,12},{... | collective-permute-start | bytes 442376 | tf_op jit(solution)/shard_map/ppermute | solution.py:18
  204.5 0.7 copy-start.4
where the time goes:
time: 296 us; the launch traced here: 292 us
  blocking collectives  111 us (38%)
  local copies, waits for them, and re-layouts  98.3 us (33%)
  matrix products  36.9 us (12%)
  other arithmetic  17.9 us (6%)
  starting transfers between devices  16.4 us (6%)
  waiting for transfers between devices  10.4 us (4%)
    all_to_all x2, blocking collectives, mirror_tile(): lax.all_to_all(first_leg, 'row', split_axis=2, concat_axis=1, tiled=True)  48.5 us
    conv_general_dilated x2, matrix products, dilated_terms(): lax.conv_general_dilated(active[None], kernel, (1, 1), 'VALID', rhs_dilat...  34.7 us
    unnamed x25, local copies, waits for them, and re-layouts  34.1 us
    all_to_all x2, blocking collectives, mirror_tile(): lax.all_to_all(output_map, 'col', split_axis=1, concat_axis=2, tiled=True)  33.4 us
    all_to_all x2, blocking collectives, mirror_tile(): lax.all_to_all(lax.all_to_all(first_leg, 'row', split_axis=2, concat_axis...  29.5 us
    all_to_all x4, local copies, waits for them, and re-layouts, mirror_tile(): lax.all_to_all(first_leg, 'row', split_axis=2, concat_axis=1, tiled=True)  12.9 us
    max x1, local copies, waits for them, and re-layouts, dilated_terms(): active = jnp.maximum(extended_input, jnp.zeros((), extended_input.dtype))  11.8 us
    ppermute x4, starting transfers between devices, padded(): before = lax.ppermute(last, axis, up)  10.8 us
  transfers between devices with their start and end apart: 8, of which 5 were waited for; matrix products, arithmetic and copies ran while one was open for 3% of the time, Pallas kernels for 0%

commit v1 on v0

v1 whole, which is shorter than its diff:
```python
import functools

import jax
import jax.numpy as jnp
from jax import lax
from jax.experimental import pallas as pl
from jax.experimental.pallas import tpu as pltpu
from jax.sharding import PartitionSpec as P

FIRST_DILATION = 8
SECOND_DILATION = 16
SIDE = 16
PACK = 8
MESH = pl.DeviceIdType.MESH
BF16 = jnp.bfloat16
F32 = jnp.float32

DIRECTIONS = ((1, 0), (-1, 0), (0, 1), (0, -1), (1, 1), (-1, 1), (1, -1), (-1, -1))


def inside(r, c, n_row, n_col):
    return (r >= 0) & (r < n_row) & (c >= 0) & (c < n_col)


def pack_sides(main, offset, side_first, side_last, groups, tc):
    @pl.loop(0, groups)
    def _(g):
        rows = [main[offset + g * PACK + k] for k in range(PACK)]
        side_first[g] = jnp.concatenate([x[:, :SIDE] for x in rows], axis=1)
        side_last[g] = jnp.concatenate([x[:, tc - SIDE :] for x in rows], axis=1)


def halo(main, left, right, side_first, side_last, d, tr, n_row, n_col, send, recv):
    r, c = lax.axis_index("row"), lax.axis_index("col")
    hg, groups = d // PACK, tr // PACK
    moves = []
    for n, (dr, dc) in enumerate(DIRECTIONS):
        if dc == 0:
            src = main.at[pl.ds(tr, d)] if dr == 1 else main.at[pl.ds(d, d)]
            dst = main.at[pl.ds(0, d)] if dr == 1 else main.at[pl.ds(tr + d, d)]
        else:
            from_ref = side_last if dc == 1 else side_first
            to_ref = left if dc == 1 else right
            if dr == 0:
                src, dst = from_ref, to_ref.at[pl.ds(hg, groups)]
            elif dr == 1:
                src, dst = from_ref.at[pl.ds(groups - hg, hg)], to_ref.at[pl.ds(0, hg)]
            else:
                src, dst = from_ref.at[pl.ds(0, hg)], to_ref.at[pl.ds(groups + hg, hg)]
        copy = pltpu.make_async_remote_copy(
            src_ref=src,
            dst_ref=dst,
            send_sem=send.at[n],
            recv_sem=recv.at[n],
            device_id=(r + dr, c + dc),
            device_id_type=MESH,
        )
        sends = inside(r + dr, c + dc, n_row, n_col)
        receives = inside(r - dr, c - dc, n_row, n_col)
        moves.append((copy, sends, receives, dst))
    return moves


def start(moves):
    for copy, sends, _, _ in moves:
        pl.when(sends)(copy.start)


def clear(moves):
    for _, _, receives, dst in moves:

        @pl.when(jnp.logical_not(receives))
        def _():
            dst[...] = jnp.zeros(dst.shape, dst.dtype)


def finish(moves):
    for copy, _, receives, _ in moves:
        pl.when(receives)(copy.wait_recv)


def finish_sends(moves):
    for copy, sends, _, _ in moves:
        pl.when(sends)(copy.wait_send)


def taps(main, left, right, weights, spread, d, tr, tc):
    height = weights.shape[0]

    @pl.loop(0, (tr + 2 * d) // PACK)
    def _(g):
        lg, rg = left[g], right[g]
        for k in range(0, PACK, 2):
            columns = []
            for u in (k, k + 1):
                x = main[g * PACK + u]
                before = jnp.concatenate(
                    [lg[:, SIDE * u + SIDE - d : SIDE * u + SIDE], x[:, : tc - d]], axis=1
                )
                after = jnp.concatenate([x[:, d:], rg[:, SIDE * u : SIDE * u + d]], axis=1)
                columns.append(jnp.concatenate([before, x, after], axis=0))
            active = jnp.maximum(jnp.concatenate(columns, axis=1), jnp.zeros((), BF16))
            out = jnp.dot(weights[...], active, preferred_element_type=F32)
            spread[g * PACK + k, :height] = out[:, :tc]
            spread[g * PACK + k + 1, :height] = out[:, tc:]


def block_rows(spread, base, row, d, ch, scale, layer):
    total = (
        spread[row, base : base + ch]
        + spread[row + d, base + ch : base + 2 * ch]
        + spread[row + 2 * d, base + 2 * ch : base + 3 * ch]
    )
    return jnp.maximum(total * scale[4 * layer] + scale[4 * layer + 2], 0.0).astype(BF16)


def kernel(
    n_row, n_col, tile, turned, w_first, w_turned, w_second, w_point, scale, out,
    fx, tx, sx, fl, fr, tl, tr_, sl, sr, ff, flast, tf, tlast, sf, slast,
    y0, mirror, spread, local, m_send, m_recv, h_send, h_recv,
):
    r, c = lax.axis_index("row"), lax.axis_index("col")
    rows, ch, tc = tile.shape
    ratio = tc // rows
    d0, d1 = FIRST_DILATION, SECOND_DILATION

    own = pltpu.make_async_copy(tile, fx.at[pl.ds(d0, rows)], local.at[0])
    own.start()

    partners = [(ratio * c + h, r // ratio) for h in range(ratio)]
    others = [(pr != r) | (pc != c) for pr, pc in partners]

    barrier = pltpu.get_barrier_semaphore()
    expected = jnp.int32(0)
    for dr, dc in DIRECTIONS:
        there = inside(r + dr, c + dc, n_row, n_col)
        expected = expected + there.astype(jnp.int32)

        @pl.when(there)
        def _():
            pl.semaphore_signal(
                barrier, inc=1, device_id=(r + dr, c + dc), device_id_type=MESH
            )

    for partner, other in zip(partners, others):
        expected = expected + other.astype(jnp.int32)

        @pl.when(other)
        def _():
            pl.semaphore_signal(barrier, inc=1, device_id=partner, device_id_type=MESH)

    pl.semaphore_wait(barrier, expected)

    mine = lax.rem(r, ratio)
    swaps = []
    for h in range(ratio):
        copy = pltpu.make_async_remote_copy(
            src_ref=turned.at[h],
            dst_ref=mirror.at[mine],
            send_sem=m_send.at[h],
            recv_sem=m_recv.at[mine],
            device_id=partners[h],
            device_id_type=MESH,
        )
        arrival = pltpu.make_async_remote_copy(
            src_ref=turned.at[h],
            dst_ref=mirror.at[h],
            send_sem=m_send.at[h],
            recv_sem=m_recv.at[h],
            device_id=partners[h],
            device_id_type=MESH,
        )
        stay = pltpu.make_async_copy(turned.at[h], mirror.at[h], local.at[1])
        pl.when(others[h])(copy.start)
        pl.when(jnp.logical_not(others[h]))(stay.start)
        swaps.append((copy, arrival, stay, others[h]))

    own.wait()
    groups = rows // PACK
    f_halo = halo(fx, fl, fr, ff, flast, d0, rows, n_row, n_col, h_send.at[0], h_recv.at[0])
    start(f_halo[:2])
    pack_sides(fx, d0, ff, flast, groups, tc)
    start(f_halo[2:])
    t_halo = halo(tx, tl, tr_, tf, tlast, d0, rows, n_row, n_col, h_send.at[1], h_recv.at[1])
    s_halo = halo(sx, sl, sr, sf, slast, d1, rows, n_row, n_col, h_send.at[2], h_recv.at[2])
    clear(f_halo)
    clear(t_halo)
    clear(s_halo)
    finish(f_halo)

    taps(fx, fl, fr, w_first, spread, d0, rows, tc)
    unroll = 4

    @pl.loop(0, rows // unroll)
    def _(t):
        hidden = [
            block_rows(spread, 0, t * unroll + u, d0, ch, scale, 0) for u in range(unroll)
        ]
        branch = jnp.dot(
            w_point[0], jnp.concatenate(hidden, axis=1), preferred_element_type=F32
        )
        for u in range(unroll):
            row = t * unroll + u
            y = branch[:, u * tc : (u + 1) * tc] * scale[1] + scale[3]
            y0[row] = (fx[d0 + row].astype(F32) + y).astype(BF16)

    for copy, arrival, stay, other in swaps:
        pl.when(other)(arrival.wait_recv)
        pl.when(jnp.logical_not(other))(stay.wait)

    half = rows // ratio

    @pl.loop(0, half)
    def _(j):
        pieces = [mirror[h, j] for h in range(ratio)]
        for k in range(ratio):
            tx[d0 + k * half + j] = jnp.concatenate(
                [x[:, k * rows : (k + 1) * rows] for x in pieces], axis=1
            )

    start(t_halo[:2])
    pack_sides(tx, d0, tf, tlast, groups, tc)
    start(t_halo[2:])
    finish(t_halo)
    taps(tx, tl, tr_, w_turned, spread, d0, rows, tc)

    @pl.loop(0, rows // unroll)
    def _(t):
        hidden = [
            block_rows(spread, 0, t * unroll + u, d0, ch, scale, 0) for u in range(unroll)
        ]
        branch = jnp.dot(
            w_point[0], jnp.concatenate(hidden, axis=1), preferred_element_type=F32
        )
        for u in range(unroll):
            row = t * unroll + u
            y = branch[:, u * tc : (u + 1) * tc] * scale[1] + scale[3]
            y = (tx[d0 + row].astype(F32) + y).astype(BF16).astype(F32)
            sx[d1 + row] = ((y + y0[row].astype(F32)) * 0.5).astype(BF16)

    start(s_halo[:2])
    pack_sides(sx, d1, sf, slast, groups, tc)
    start(s_halo[2:])
    finish(s_halo)
    taps(sx, sl, sr, w_second, spread, d1, rows, tc)

    @pl.loop(0, rows // 2)
    def _(t):
        hidden = [
            block_rows(spread, base, t * 2 + u, d1, ch, scale, 1)
            for u in range(2)
            for base in (0, 3 * ch)
        ]
        branch = jnp.dot(
            w_point[1], jnp.concatenate(hidden, axis=1), preferred_element_type=F32
        )
        for u in range(2):
            row = t * 2 + u
            x = sx[d1 + row].astype(F32)
            both = []
            for v in (2 * u, 2 * u + 1):
                y = branch[:, v * tc : (v + 1) * tc] * scale[5] + scale[7]
                both.append((x + y).astype(BF16).astype(F32))
            out[row] = ((both[0] + both[1]) * 0.5).astype(BF16)

    for copy, arrival, stay, other in swaps:
        pl.when(other)(copy.wait_send)
    finish_sends(f_halo)
    finish_sends(t_halo)
    finish_sends(s_halo)


def body(features, w_dilated, w_pointwise, norm_gain, norm_bias):
    n_row, n_col = lax.axis_size("row"), lax.axis_size("col")
    ch, rows, tc = features.shape
    ratio = tc // rows
    half = rows // ratio
    tile = jnp.transpose(features, (1, 0, 2))
    turned = jnp.transpose(
        features.reshape(ch, rows, ratio, ratio, half), (2, 4, 0, 3, 1)
    ).reshape(ratio, half, ch, tc)
    straight = jnp.transpose(w_dilated, (0, 1, 3, 2, 4)).reshape(2, 3 * ch, 3 * ch)
    swapped = jnp.transpose(w_dilated, (0, 2, 3, 1, 4)).reshape(2, 3 * ch, 3 * ch)
    second = jnp.concatenate([straight[1], swapped[1]], axis=0)
    scale = jnp.concatenate([norm_gain, norm_bias], axis=1).reshape(8, ch, 1)
    scale = jnp.broadcast_to(scale, (8, ch, tc))
    d0, d1 = FIRST_DILATION, SECOND_DILATION
    groups = rows // PACK

    def vmem(*shape, dtype=BF16):
        return pltpu.VMEM(shape, dtype)

    def border(d):
        return vmem(groups + 2 * d // PACK, ch, tc)

    result = pl.pallas_call(
        functools.partial(kernel, n_row, n_col),
        out_shape=jax.ShapeDtypeStruct((rows, ch, tc), BF16),
        in_specs=[pl.BlockSpec(memory_space=pl.ANY)] * 2
        + [pl.BlockSpec(memory_space=pltpu.VMEM)] * 5,
        out_specs=pl.BlockSpec(memory_space=pltpu.VMEM),
        scratch_shapes=[
            vmem(rows + 2 * d0, ch, tc),
            vmem(rows + 2 * d0, ch, tc),
            vmem(rows + 2 * d1, ch, tc),
            border(d0), border(d0), border(d0), border(d0), border(d1), border(d1),
            *[vmem(groups, ch, tc) for _ in range(6)],
            vmem(rows, ch, tc),
            vmem(ratio, half, ch, tc),
            vmem(rows + 2 * d1, 6 * ch, tc, dtype=F32),
            pltpu.SemaphoreType.DMA((2,)),
            pltpu.SemaphoreType.DMA((ratio,)),
            pltpu.SemaphoreType.DMA((ratio,)),
            pltpu.SemaphoreType.DMA((3, 8)),
            pltpu.SemaphoreType.DMA((3, 8)),
        ],
        compiler_params=pltpu.CompilerParams(
            collective_id=0, has_side_effects=True, vmem_limit_bytes=48 * 1024 * 1024
        ),
        cost_estimate=pl.CostEstimate(
            flops=4 * 2 * 9 * ch * ch * rows * tc, bytes_accessed=6 * ch * rows * tc, transcendentals=0
        ),
    )(tile, turned, straight[0], swapped[0], second, w_pointwise, scale)
    return jnp.transpose(result, (1, 0, 2))


def solution(mesh):
    in_specs = (P(None, "row", "col"), P(), P(), P(), P())
    out_specs = P(None, "row", "col")
    return jax.shard_map(body, mesh=mesh, in_specs=in_specs, out_specs=out_specs, check_vma=False)
```

time: 296 us -> 93.3 us (0.32)
  the two profiles are of different devices: /device:TPU:0 before, /device:TPU:11 now
where the time goes in v1:
time: 93.3 us; the launch traced here: 93.2 us
  Pallas kernels  83.6 us (90%)
  local copies, waits for them, and re-layouts  9.36 us (10%)
    pallas_call x1, Pallas kernels, body(): pl.pallas_call(functools.partial(kernel, n_row, n_col), out_shape=jax.Sha...  83.6 us
    transpose x1, local copies, waits for them, and re-layouts, body(): jnp.transpose(features.reshape(ch, rows, ratio, ratio, half), (2, 4, 0, 3...  2.62 us
    slice x4, local copies, waits for them, and re-layouts, body(): second = jnp.concatenate([straight[1], swapped[1]], axis=0)  2.12 us
    unnamed x10, local copies, waits for them, and re-layouts  2.08 us

profile of v1, /device:TPU:11, one launch (start us, length us, event | category | flops | bytes accessed | tf_op | source)
XLA Modules:
  0.0 93.2 jit_solution(1487932430372357557)
XLA Ops:
  0.0 0.0 copy-start.1
  0.0 1.0 %fusion = (bf16[1,3,48,3,48]{4,2,3,1,0:T(8,128)(2,1)S(1)}, bf16[1,3,48,3,48]{4,2,3,1,0:T(8,128)(2,1)S(1)}) fusion(bf16[2,3,48,3,48]{4,2,3,1,0:T(8,128)(2,1)} %bitcast.13), kind=kLoop, calls=%fused_computation.3 | loop fusion | bytes 165888 | tf_op jit(solution)/shard_map/slice | solution.py:284
  1.0 0.1 copy.18
  1.1 0.1 squeeze.14
  1.2 1.0 %fusion.1 = (bf16[1,3,48,3,48]{4,2,1,3,0:T(8,128)(2,1)S(1)}, bf16[1,3,48,3,48]{4,2,1,3,0:T(8,128)(2,1)S(1)}) fusion(bf16[2,3,48,3,48]{4,2,1,3,0:T(8,128)(2,1)} %bitcast.14), kind=kLoop, calls=%fused_computation.4 | loop fusion | bytes 165888 | tf_op jit(solution)/shard_map/slice | solution.py:284
  2.2 0.1 copy.19
  2.3 0.1 squeeze.15
  2.4 0.1 copy.16
  2.5 0.1 squeeze.12.w_first
  2.6 0.1 copy.17
  2.7 0.1 squeeze.13.w_turned
  2.8 0.0 copy-done.1
  2.8 1.5 %copy.14 = bf16[48,64,128]{1,2,0:T(8,128)(2,1)} copy(bf16[48,64,128]{2,1,0:T(8,128)(2,1)S(1)} %copy-done.1) | data formatting | bytes 1572864 | tf_op args[0]
  4.4 2.6 %copy.15 = bf16[2,32,48,2,64]{4,3,2,1,0:T(2,128)(2,1)S(1)} copy(bf16[2,32,48,2,64]{4,1,3,0,2:T(8,128)(2,1)} %bitcast.12) | data formatting | bytes 1572864 | tf_op jit(solution)/shard_map/transpose | solution.py:279
  7.0 0.0 copy-start.2
  7.0 0.0 copy-start.3
  7.0 0.0 copy-start
  7.0 0.8 reshape.19.turned
  7.8 0.5 copy.22
  8.3 0.0 copy-done.2
  8.3 0.0 copy-done.3
  8.4 0.1 broadcast_in_dim.8.scale
  8.5 0.0 copy-done
  8.5 83.6 %shard_map.55 = bf16[64,48,128]{2,1,0:T(8,128)(2,1)S(1)} custom-call(bf16[64,48,128]{2,1,0:T(8,128)(2,1)S(1)} %bitcast.10, bf16[2,32,48,128]{3,2,1,0:T(8,128)(2,1)S(1)} %reshape.19.turned, bf16[144,144]{1,0:T(8,128)(2,1)S(1)} %squeeze.12.w_first, bf16[144,144]{1,0:T(8,128)(2,1)S(1)} %squeeze.13.w_turned, bf16[288,144]{1,0:T(8,128)(2,1)S(1)} %pad_maximum_fusion.w_second, ...), custom_call_target="tpu_custom_call" | custom-call | flops 1358954496 | bytes 2359296 | tf_op jit(solution)/shard_map/pallas_call | solution.py:296
  92.1 1.1 %copy.20 = bf16[48,64,128]{2,1,0:T(8,128)(2,1)} copy(bf16[48,64,128]{2,0,1:T(8,128)(2,1)S(1)} %bitcast.11) | data formatting | bytes 1572864 | tf_op jit(solution)/shard_map/transpose | solution.py:324
  (2 shorter events, 0.0 us)
Async XLA Ops:
  0.0 2.8 %copy-start.1 = (bf16[48,64,128]{2,1,0:T(8,128)(2,1)S(1)}, bf16[48,64,128]{2,1,0:T(8,128)(2,1)}, u32[]{:S(2)}) copy-start(bf16[48,64,128]{2,1,0:T(8,128)(2,1)} %param.5) | copy-start | bytes 2359300
  7.0 1.3 %copy-start.2 = (f32[2,2,48]{2,1,0:T(2,128)S(1)}, f32[2,2,48]{2,1,0:T(2,128)}, u32[]{:S(2)}) copy-start(f32[2,2,48]{2,1,0:T(2,128)} %param.9) | copy-start | bytes 2308
  7.0 1.3 %copy-start.3 = (f32[2,2,48]{2,1,0:T(2,128)S(1)}, f32[2,2,48]{2,1,0:T(2,128)}, u32[]{:S(2)}) copy-start(f32[2,2,48]{2,1,0:T(2,128)} %param.8) | copy-start | bytes 2308
  7.0 1.4 %copy-start = (bf16[2,48,48]{2,1,0:T(8,128)(2,1)S(1)}, bf16[2,48,48]{2,1,0:T(8,128)(2,1)}, u32[]{:S(2)}) copy-start(bf16[2,48,48]{2,1,0:T(8,128)(2,1)} %w_point.1) | copy-start | bytes 27652

commit v2 on v1

--- a/solution.py
+++ b/solution.py
@@ -114,10 +114,173 @@
     return jnp.maximum(total * scale[4 * layer] + scale[4 * layer + 2], 0.0).astype(BF16)
 
 
+def fill_weights(w_taps, w_first, w_turned, w_second, ch):
+    for p in range(3):
+        for q in range(3):
+            for layer, ref, base, tap in (
+                (0, w_first, 0, 3 * p + q),
+                (0, w_turned, 0, 3 * q + p),
+                (1, w_second, 0, 3 * p + q),
+                (1, w_second, 3 * ch, 3 * q + p),
+            ):
+                ref[base + p * ch : base + (p + 1) * ch, q * ch : (q + 1) * ch] = w_taps[
+                    9 * layer + tap
+                ]
+
+
+class Swap:
+    def __init__(
+        self, n_row, n_col, ratio, parcel, mirror, relay, local, m_send, m_recv, l_send, l_recv
+    ):
+        r, c = lax.axis_index("row"), lax.axis_index("col")
+        self.me = (r, c)
+        self.ratio = ratio
+        self.local = local
+        self.cut = parcel.shape[1] // 2
+        mine = lax.rem(r, ratio)
+        big = r // ratio
+        odd, base = lax.rem(c, 2), c // 2
+        slots = n_col // 2
+        same = lambda a, b: (a[0] == b[0]) & (a[1] == b[1])
+        part = lambda ref, piece: ref.at[pl.ds(piece * self.cut, self.cut)]
+
+        def remote(src, dst, send, recv, to):
+            return pltpu.make_async_remote_copy(
+                src_ref=src, dst_ref=dst, send_sem=send, recv_sem=recv,
+                device_id=to, device_id_type=MESH,
+            )
+
+        self.out = []
+        for piece in (0, 1):
+            for h in range(ratio):
+                goal = (ratio * c + h, big)
+                if piece == 0:
+                    via = (ratio * c + mine, 2 * base + lax.rem(big, 2))
+                    slot = (big // 2) * ratio + h
+                else:
+                    via = (ratio * big + h, 2 * (big // 2) + odd)
+                    slot = base * ratio + mine
+                stays = same(goal, self.me)
+                short = same(via, goal) | same(via, self.me)
+                src = part(parcel.at[h], piece)
+                straight = remote(
+                    src, part(mirror.at[mine], piece),
+                    m_send.at[piece, h], m_recv.at[piece, mine], goal,
+                )
+                bent = remote(
+                    src, relay.at[piece, slot],
+                    m_send.at[piece, h], l_recv.at[piece, slot], via,
+                )
+                keep = pltpu.make_async_copy(
+                    src, part(mirror.at[h], piece), local.at[1 + piece]
+                )
+                arrival = remote(
+                    src, part(mirror.at[h], piece),
+                    m_send.at[piece, h], m_recv.at[piece, h], goal,
+                )
+                no = jnp.logical_not
+                self.out.append(
+                    dict(
+                        goal=goal, via=via, piece=piece, h=h, stays=stays,
+                        straight=no(stays) & short, bent=no(stays) & no(short),
+                        straight_copy=straight, bent_copy=bent, keep=keep, arrival=arrival,
+                    )
+                )
+
+        self.through = []
+        relays = (big // 2) == base
+        for piece in (0, 1):
+            for m in range(slots):
+                for k in range(ratio):
+                    if piece == 0:
+                        source = (ratio * (2 * m + odd) + mine, big)
+                        goal = (ratio * big + k, 2 * m + odd)
+                        h = k
+                    else:
+                        source = (ratio * big + k, 2 * m + odd)
+                        goal = (ratio * (2 * m + odd) + mine, big)
+                        h = mine
+                    theirs = lax.rem(source[0], ratio)
+                    slot = m * ratio + k
+                    when = (
+                        relays
+                        & jnp.logical_not(same(source, self.me))
+                        & jnp.logical_not(same(goal, self.me))
+                        & jnp.logical_not(same(goal, source))
+                    )
+                    copy = remote(
+                        relay.at[piece, slot], part(mirror.at[theirs], piece),
+                        l_send.at[piece, slot], m_recv.at[piece, theirs], goal,
+                    )
+                    arrival = remote(
+                        relay.at[piece, slot], relay.at[piece, slot],
+                        l_send.at[piece, slot], l_recv.at[piece, slot], source,
+                    )
+                    self.through.append((piece, when, source, copy, arrival))
+
+        self.into = []
+        for piece in (0, 1):
+            for h in range(ratio):
+                source = (ratio * c + h, big)
+                sb, so = source[0] // ratio, lax.rem(source[0], ratio)
+                if piece == 0:
+                    via = (ratio * big + so, 2 * (big // 2) + lax.rem(sb, 2))
+                else:
+                    via = (ratio * sb + mine, 2 * (sb // 2) + lax.rem(big, 2))
+                stays = same(source, self.me)
+                short = same(via, source) | same(via, self.me)
+                self.into.append((source, via, stays, short))
+
+    def greet(self, barrier, expected):
+        def signal(when, to):
+            @pl.when(when)
+            def _():
+                pl.semaphore_signal(barrier, inc=1, device_id=to, device_id_type=MESH)
+
+        for source, via, stays, short in self.into:
+            no = jnp.logical_not
+            signal(no(stays) & short, source)
+            signal(no(stays) & no(short), via)
+        for _, when, source, _, _ in self.through:
+            signal(when, source)
+            expected = expected + when.astype(jnp.int32)
+        for x in self.out:
+            expected = expected + jnp.logical_not(x["stays"]).astype(jnp.int32)
+        return expected
+
+    def start(self):
+        for x in self.out:
+            pl.when(x["bent"])(x["bent_copy"].start)
+        for x in self.out:
+            pl.when(x["straight"])(x["straight_copy"].start)
+            pl.when(x["stays"])(x["keep"].start)
+
+    def forward(self, piece):
+        for at, when, _, copy, arrival in self.through:
+            if at == piece:
+
+                @pl.when(when)
+                def _():
+                    arrival.wait_recv()
+                    copy.start()
+
+    def arrive(self):
+        for x in self.out:
+            pl.when(jnp.logical_not(x["stays"]))(x["arrival"].wait_recv)
+            pl.when(x["stays"])(x["keep"].wait)
+
+    def finish(self):
+        for x in self.out:
+            pl.when(jnp.logical_not(x["stays"]))(x["straight_copy"].wait_send)
+        for _, when, _, copy, _ in self.through:
+            pl.when(when)(copy.wait_send)
+
+
 def kernel(
-    n_row, n_col, tile, turned, w_first, w_turned, w_second, w_point, scale, out,
+    n_row, n_col, tile, turned, w_taps, w_point, scale, out,
     fx, tx, sx, fl, fr, tl, tr_, sl, sr, ff, flast, tf, tlast, sf, slast,
-    y0, mirror, spread, local, m_send, m_recv, h_send, h_recv,
+    y0, parcel, mirror, relay, w_first, w_turned, w_second, spread,
+    local, m_send, m_recv, l_send, l_recv, h_send, h_recv,
 ):
     r, c = lax.axis_index("row"), lax.axis_index("col")
     rows, ch, tc = tile.shape
@@ -127,8 +290,7 @@
     own = pltpu.make_async_copy(tile, fx.at[pl.ds(d0, rows)], local.at[0])
     own.start()
 
-    partners = [(ratio * c + h, r // ratio) for h in range(ratio)]
-    others = [(pr != r) | (pc != c) for pr, pc in partners]
+    swap = Swap(n_row, n_col, ratio, parcel, mirror, relay, local, m_send, m_recv, l_send, l_recv)
 
     barrier = pltpu.get_barrier_semaphore()
     expected = jnp.int32(0)
@@ -142,38 +304,19 @@
                 barrier, inc=1, device_id=(r + dr, c + dc), device_id_type=MESH
             )
 
-    for partner, other in zip(partners, others):
-        expected = expected + other.astype(jnp.int32)
-
-        @pl.when(other)
-        def _():
-            pl.semaphore_signal(barrier, inc=1, device_id=partner, device_id_type=MESH)
+    expected = swap.greet(barrier, expected)
+
+    half = rows // ratio
+
+    @pl.loop(0, half)
+    def _(j):
+        for h in range(ratio):
+            pair = [turned[h * rows + ratio * j + k] for k in range(ratio)]
+            parcel[h, j] = jnp.concatenate(pair, axis=1)
 
     pl.semaphore_wait(barrier, expected)
 
-    mine = lax.rem(r, ratio)
-    swaps = []
-    for h in range(ratio):
-        copy = pltpu.make_async_remote_copy(
-            src_ref=turned.at[h],
-            dst_ref=mirror.at[mine],
-            send_sem=m_send.at[h],
-            recv_sem=m_recv.at[mine],
-            device_id=partners[h],
-            device_id_type=MESH,
-        )
-        arrival = pltpu.make_async_remote_copy(
-            src_ref=turned.at[h],
-            dst_ref=mirror.at[h],
-            send_sem=m_send.at[h],
-            recv_sem=m_recv.at[h],
-            device_id=partners[h],
-            device_id_type=MESH,
-        )
-        stay = pltpu.make_async_copy(turned.at[h], mirror.at[h], local.at[1])
-        pl.when(others[h])(copy.start)
-        pl.when(jnp.logical_not(others[h]))(stay.start)
-        swaps.append((copy, arrival, stay, others[h]))
+    swap.start()
 
     own.wait()
     groups = rows // PACK
@@ -186,6 +329,8 @@
     clear(f_halo)
     clear(t_halo)
     clear(s_halo)
+    fill_weights(w_taps, w_first, w_turned, w_second, ch)
+    swap.forward(1)
     finish(f_halo)
 
     taps(fx, fl, fr, w_first, spread, d0, rows, tc)
@@ -204,17 +349,14 @@
             y = branch[:, u * tc : (u + 1) * tc] * scale[1] + scale[3]
             y0[row] = (fx[d0 + row].astype(F32) + y).astype(BF16)
 
-    for copy, arrival, stay, other in swaps:
-        pl.when(other)(arrival.wait_recv)
-        pl.when(jnp.logical_not(other))(stay.wait)
-
-    half = rows // ratio
+    swap.forward(0)
+    swap.arrive()
 
     @pl.loop(0, half)
     def _(j):
         pieces = [mirror[h, j] for h in range(ratio)]
         for k in range(ratio):
-            tx[d0 + k * half + j] = jnp.concatenate(
+            tx[d0 + ratio * j + k] = jnp.concatenate(
                 [x[:, k * rows : (k + 1) * rows] for x in pieces], axis=1
             )
 
@@ -263,8 +405,7 @@
                 both.append((x + y).astype(BF16).astype(F32))
             out[row] = ((both[0] + both[1]) * 0.5).astype(BF16)
 
-    for copy, arrival, stay, other in swaps:
-        pl.when(other)(copy.wait_send)
+    swap.finish()
     finish_sends(f_halo)
     finish_sends(t_halo)
     finish_sends(s_halo)
@@ -275,13 +416,10 @@
     ch, rows, tc = features.shape
     ratio = tc // rows
     half = rows // ratio
+    slots = ratio * (n_col // 2)
     tile = jnp.transpose(features, (1, 0, 2))
-    turned = jnp.transpose(
-        features.reshape(ch, rows, ratio, ratio, half), (2, 4, 0, 3, 1)
-    ).reshape(ratio, half, ch, tc)
-    straight = jnp.transpose(w_dilated, (0, 1, 3, 2, 4)).reshape(2, 3 * ch, 3 * ch)
-    swapped = jnp.transpose(w_dilated, (0, 2, 3, 1, 4)).reshape(2, 3 * ch, 3 * ch)
-    second = jnp.concatenate([straight[1], swapped[1]], axis=0)
+    turned = jnp.transpose(features, (2, 0, 1))
+    w_taps = w_dilated.reshape(-1, ch, ch)
     scale = jnp.concatenate([norm_gain, norm_bias], axis=1).reshape(8, ch, 1)
     scale = jnp.broadcast_to(scale, (8, ch, tc))
     d0, d1 = FIRST_DILATION, SECOND_DILATION
@@ -296,8 +434,8 @@
     result = pl.pallas_call(
         functools.partial(kernel, n_row, n_col),
         out_shape=jax.ShapeDtypeStruct((rows, ch, tc), BF16),
-        in_specs=[pl.BlockSpec(memory_space=pl.ANY)] * 2
-        + [pl.BlockSpec(memory_space=pltpu.VMEM)] * 5,
+        in_specs=[pl.BlockSpec(memory_space=pl.ANY)]
+        + [pl.BlockSpec(memory_space=pltpu.VMEM)] * 4,
         out_specs=pl.BlockSpec(memory_space=pltpu.VMEM),
         scratch_shapes=[
             vmem(rows + 2 * d0, ch, tc),
@@ -307,10 +445,17 @@
             *[vmem(groups, ch, tc) for _ in range(6)],
             vmem(rows, ch, tc),
             vmem(ratio, half, ch, tc),
+            vmem(ratio, half, ch, tc),
+            vmem(2, slots, half // 2, ch, tc),
+            vmem(3 * ch, 3 * ch),
+            vmem(3 * ch, 3 * ch),
+            vmem(6 * ch, 3 * ch),
             vmem(rows + 2 * d1, 6 * ch, tc, dtype=F32),
-            pltpu.SemaphoreType.DMA((2,)),
-            pltpu.SemaphoreType.DMA((ratio,)),
-            pltpu.SemaphoreType.DMA((ratio,)),
+            pltpu.SemaphoreType.DMA((3,)),
+            pltpu.SemaphoreType.DMA((2, ratio)),
+            pltpu.SemaphoreType.DMA((2, ratio)),
+            pltpu.SemaphoreType.DMA((2, slots)),
+            pltpu.SemaphoreType.DMA((2, slots)),
             pltpu.SemaphoreType.DMA((3, 8)),
             pltpu.SemaphoreType.DMA((3, 8)),
         ],
@@ -320,7 +465,7 @@
         cost_estimate=pl.CostEstimate(
             flops=4 * 2 * 9 * ch * ch * rows * tc, bytes_accessed=6 * ch * rows * tc, transcendentals=0
         ),
-    )(tile, turned, straight[0], swapped[0], second, w_pointwise, scale)
+    )(tile, turned, w_taps, w_pointwise, scale)
     return jnp.transpose(result, (1, 0, 2))
 
 

time: 93.3 us -> 84.7 us (0.908)
  the two profiles are of different devices: /device:TPU:11 before, /device:TPU:9 now
where the time goes in v2:
time: 84.7 us; the launch traced here: 84.5 us
  Pallas kernels  79 us (93%)
  local copies, waits for them, and re-layouts  4.78 us (6%)
    pallas_call x1, Pallas kernels, body(): pl.pallas_call(functools.partial(kernel, n_row, n_col), out_shape=jax.Sha...  79 us
    unnamed x6, local copies, waits for them, and re-layouts  3.59 us

profile of v2, /device:TPU:9, one launch (start us, length us, event | category | flops | bytes accessed | tf_op | source)
XLA Modules:
  0.0 84.5 jit_solution(12235207436986697152)
XLA Ops:
  0.0 0.7 pad_maximum_fusion
  0.7 0.1 broadcast_in_dim.8.scale
  0.8 1.6 %copy.10 = bf16[48,64,128]{2,0,1:T(8,128)(2,1)S(1)} copy(bf16[48,64,128]{2,1,0:T(8,128)(2,1)} %param.5) | data formatting | bytes 1572864 | tf_op args[0]
  2.5 0.0 copy-start
  2.5 0.0 copy-start.1
  2.5 1.9 %copy.7 = bf16[48,64,128]{1,0,2:T(8,128)(2,1)S(1)} copy(bf16[48,64,128]{2,1,0:T(8,128)(2,1)} %param.5) | data formatting | bytes 1572864 | tf_op args[0]
  4.4 0.0 copy-done
  4.4 0.0 copy-done.1
  4.5 79.0 %shard_map.55 = bf16[64,48,128]{2,1,0:T(8,128)(2,1)S(1)} custom-call(bf16[64,48,128]{2,1,0:T(8,128)(2,1)S(1)} %bitcast.9, bf16[128,48,64]{2,1,0:T(8,128)(2,1)S(1)} %bitcast.7, bf16[18,48,48]{2,1,0:T(8,128)(2,1)S(1)} %bitcast.10, bf16[2,48,48]{2,1,0:T(8,128)(2,1)S(1)} %copy-done.1, f32[8,48,128]{2,1,0:T(8,128)S(1)} %broadcast_in_dim.8.scale), custom_call_target="tpu_custom_call" | custom-call | flops 1358954496 | bytes 2359296 | tf_op jit(solution)/shard_map/pallas_call | solution.py:434
  83.5 1.1 %copy.8 = bf16[48,64,128]{2,1,0:T(8,128)(2,1)} copy(bf16[48,64,128]{2,0,1:T(8,128)(2,1)S(1)} %bitcast.8) | data formatting | bytes 1572864 | tf_op jit(solution)/shard_map/transpose | solution.py:469
Async XLA Ops:
  2.5 2.0 %copy-start = (bf16[2,3,3,48,48]{4,3,2,1,0:T(8,128)(2,1)S(1)}, bf16[2,3,3,48,48]{4,3,2,1,0:T(8,128)(2,1)}, u32[]{:S(2)}) copy-start(bf16[2,3,3,48,48]{4,3,2,1,0:T(8,128)(2,1)} %param.6) | copy-start | bytes 248836
  2.5 2.0 %copy-start.1 = (bf16[2,48,48]{2,1,0:T(8,128)(2,1)S(1)}, bf16[2,48,48]{2,1,0:T(8,128)(2,1)}, u32[]{:S(2)}) copy-start(bf16[2,48,48]{2,1,0:T(8,128)(2,1)} %w_point.1) | copy-start | bytes 27652

commit v3 on v2

--- a/solution.py
+++ b/solution.py
@@ -84,48 +84,60 @@
         pl.when(sends)(copy.wait_send)
 
 
-def taps(main, left, right, weights, spread, d, tr, tc):
-    height = weights.shape[0]
-
-    @pl.loop(0, (tr + 2 * d) // PACK)
+def shift_rows(main, lanes, first, count, d, ch, tc):
+    @pl.loop(0, count // PACK)
     def _(g):
-        lg, rg = left[g], right[g]
-        for k in range(0, PACK, 2):
-            columns = []
-            for u in (k, k + 1):
-                x = main[g * PACK + u]
-                before = jnp.concatenate(
-                    [lg[:, SIDE * u + SIDE - d : SIDE * u + SIDE], x[:, : tc - d]], axis=1
-                )
-                after = jnp.concatenate([x[:, d:], rg[:, SIDE * u : SIDE * u + d]], axis=1)
-                columns.append(jnp.concatenate([before, x, after], axis=0))
-            active = jnp.maximum(jnp.concatenate(columns, axis=1), jnp.zeros((), BF16))
-            out = jnp.dot(weights[...], active, preferred_element_type=F32)
-            spread[g * PACK + k, :height] = out[:, :tc]
-            spread[g * PACK + k + 1, :height] = out[:, tc:]
-
-
-def block_rows(spread, base, row, d, ch, scale, layer):
-    total = (
-        spread[row, base : base + ch]
-        + spread[row + d, base + ch : base + 2 * ch]
-        + spread[row + 2 * d, base + 2 * ch : base + 3 * ch]
+        for k in range(PACK):
+            e = first + g * PACK + k
+            x = jnp.maximum(main[e], jnp.zeros((), BF16))
+            lanes[e, :ch] = jnp.concatenate([x[:, tc - d :], x[:, : tc - d]], axis=1)
+            lanes[e, ch : 2 * ch] = x
+            lanes[e, 2 * ch :] = jnp.concatenate([x[:, d:], x[:, :d]], axis=1)
+
+
+def patch_sides(left, right, lanes, groups, d, ch, tc):
+    @pl.loop(0, groups)
+    def _(g):
+        lg = jnp.maximum(left[g], jnp.zeros((), BF16))
+        rg = jnp.maximum(right[g], jnp.zeros((), BF16))
+        for k in range(PACK):
+            at = SIDE * k
+            lanes[g * PACK + k, :ch, :d] = lg[:, at + SIDE - d : at + SIDE]
+            lanes[g * PACK + k, 2 * ch :, tc - d :] = rg[:, at : at + d]
+
+
+def border_rows(main, left, right, lanes, rows, d, ch, tc):
+    shift_rows(main, lanes, 0, d, d, ch, tc)
+    shift_rows(main, lanes, rows + d, d, d, ch, tc)
+    patch_sides(left, right, lanes, (rows + 2 * d) // PACK, d, ch, tc)
+
+
+def hidden_rows(lanes, weights, row, count, d, ch, tc, scale, layer):
+    columns = [
+        jnp.concatenate([lanes[row + u + p * d] for p in range(3)], axis=0) for u in range(count)
+    ]
+    total = jnp.dot(
+        weights[...], jnp.concatenate(columns, axis=1), preferred_element_type=F32
     )
-    return jnp.maximum(total * scale[4 * layer] + scale[4 * layer + 2], 0.0).astype(BF16)
+    sets = []
+    for base in range(0, weights.shape[0], ch):
+        parts = [
+            total[base : base + ch, u * tc : (u + 1) * tc] * scale[4 * layer]
+            + scale[4 * layer + 2]
+            for u in range(count)
+        ]
+        sets += [jnp.maximum(x, 0.0).astype(BF16) for x in parts]
+    return jnp.concatenate(sets, axis=1)
 
 
 def fill_weights(w_taps, w_first, w_turned, w_second, ch):
     for p in range(3):
         for q in range(3):
-            for layer, ref, base, tap in (
-                (0, w_first, 0, 3 * p + q),
-                (0, w_turned, 0, 3 * q + p),
-                (1, w_second, 0, 3 * p + q),
-                (1, w_second, 3 * ch, 3 * q + p),
-            ):
-                ref[base + p * ch : base + (p + 1) * ch, q * ch : (q + 1) * ch] = w_taps[
-                    9 * layer + tap
-                ]
+            at = (3 * p + q) * ch
+            w_first[:, at : at + ch] = w_taps[3 * p + q]
+            w_turned[:, at : at + ch] = w_taps[3 * q + p]
+            w_second[:ch, at : at + ch] = w_taps[9 + 3 * p + q]
+            w_second[ch:, at : at + ch] = w_taps[9 + 3 * q + p]
 
 
 class Swap:
@@ -279,7 +291,7 @@
 def kernel(
     n_row, n_col, tile, turned, w_taps, w_point, scale, out,
     fx, tx, sx, fl, fr, tl, tr_, sl, sr, ff, flast, tf, tlast, sf, slast,
-    y0, parcel, mirror, relay, w_first, w_turned, w_second, spread,
+    y0, parcel, mirror, relay, w_first, w_turned, w_second, lanes,
     local, m_send, m_recv, l_send, l_recv, h_send, h_recv,
 ):
     r, c = lax.axis_index("row"), lax.axis_index("col")
@@ -331,19 +343,15 @@
     clear(s_halo)
     fill_weights(w_taps, w_first, w_turned, w_second, ch)
     swap.forward(1)
+    shift_rows(fx, lanes, d0, rows, d0, ch, tc)
     finish(f_halo)
-
-    taps(fx, fl, fr, w_first, spread, d0, rows, tc)
+    border_rows(fx, fl, fr, lanes, rows, d0, ch, tc)
     unroll = 4
 
     @pl.loop(0, rows // unroll)
     def _(t):
-        hidden = [
-            block_rows(spread, 0, t * unroll + u, d0, ch, scale, 0) for u in range(unroll)
-        ]
-        branch = jnp.dot(
-            w_point[0], jnp.concatenate(hidden, axis=1), preferred_element_type=F32
-        )
+        hidden = hidden_rows(lanes, w_first, t * unroll, unroll, d0, ch, tc, scale, 0)
+        branch = jnp.dot(w_point[0], hidden, preferred_element_type=F32)
         for u in range(unroll):
             row = t * unroll + u
             y = branch[:, u * tc : (u + 1) * tc] * scale[1] + scale[3]
@@ -363,17 +371,14 @@
     start(t_halo[:2])
     pack_sides(tx, d0, tf, tlast, groups, tc)
     start(t_halo[2:])
+    shift_rows(tx, lanes, d0, rows, d0, ch, tc)
     finish(t_halo)
-    taps(tx, tl, tr_, w_turned, spread, d0, rows, tc)
+    border_rows(tx, tl, tr_, lanes, rows, d0, ch, tc)
 
     @pl.loop(0, rows // unroll)
     def _(t):
-        hidden = [
-            block_rows(spread, 0, t * unroll + u, d0, ch, scale, 0) for u in range(unroll)
-        ]
-        branch = jnp.dot(
-            w_point[0], jnp.concatenate(hidden, axis=1), preferred_element_type=F32
-        )
+        hidden = hidden_rows(lanes, w_turned, t * unroll, unroll, d0, ch, tc, scale, 0)
+        branch = jnp.dot(w_point[0], hidden, preferred_element_type=F32)
         for u in range(unroll):
             row = t * unroll + u
             y = branch[:, u * tc : (u + 1) * tc] * scale[1] + scale[3]
@@ -383,24 +388,19 @@
     start(s_halo[:2])
     pack_sides(sx, d1, sf, slast, groups, tc)
     start(s_halo[2:])
+    shift_rows(sx, lanes, d1, rows, d1, ch, tc)
     finish(s_halo)
-    taps(sx, sl, sr, w_second, spread, d1, rows, tc)
-
-    @pl.loop(0, rows // 2)
+    border_rows(sx, sl, sr, lanes, rows, d1, ch, tc)
+
+    @pl.loop(0, rows // unroll)
     def _(t):
-        hidden = [
-            block_rows(spread, base, t * 2 + u, d1, ch, scale, 1)
-            for u in range(2)
-            for base in (0, 3 * ch)
-        ]
-        branch = jnp.dot(
-            w_point[1], jnp.concatenate(hidden, axis=1), preferred_element_type=F32
-        )
-        for u in range(2):
-            row = t * 2 + u
+        hidden = hidden_rows(lanes, w_second, t * unroll, unroll, d1, ch, tc, scale, 1)
+        branch = jnp.dot(w_point[1], hidden, preferred_element_type=F32)
+        for u in range(unroll):
+            row = t * unroll + u
             x = sx[d1 + row].astype(F32)
             both = []
-            for v in (2 * u, 2 * u + 1):
+            for v in (u, u + unroll):
                 y = branch[:, v * tc : (v + 1) * tc] * scale[5] + scale[7]
                 both.append((x + y).astype(BF16).astype(F32))
             out[row] = ((both[0] + both[1]) * 0.5).astype(BF16)
@@ -447,10 +447,10 @@
             vmem(ratio, half, ch, tc),
             vmem(ratio, half, ch, tc),
             vmem(2, slots, half // 2, ch, tc),
-            vmem(3 * ch, 3 * ch),
-            vmem(3 * ch, 3 * ch),
-            vmem(6 * ch, 3 * ch),
-            vmem(rows + 2 * d1, 6 * ch, tc, dtype=F32),
+            vmem(ch, 9 * ch),
+            vmem(ch, 9 * ch),
+            vmem(2 * ch, 9 * ch),
+            vmem(rows + 2 * d1, 3 * ch, tc),
             pltpu.SemaphoreType.DMA((3,)),
             pltpu.SemaphoreType.DMA((2, ratio)),
             pltpu.SemaphoreType.DMA((2, ratio)),

time: 84.7 us -> 85.1 us (level)
  no operation moved by 1% of the time
where the time goes in v3:
time: 85.1 us; the launch traced here: 84.9 us
  Pallas kernels  79.4 us (93%)
  local copies, waits for them, and re-layouts  4.78 us (6%)
    pallas_call x1, Pallas kernels, body(): pl.pallas_call(functools.partial(kernel, n_row, n_col), out_shape=jax.Sha...  79.4 us
    unnamed x6, local copies, waits for them, and re-layouts  3.59 us

profile of v3, /device:TPU:9, one launch (start us, length us, event | category | flops | bytes accessed | tf_op | source)
XLA Modules:
  0.0 84.9 jit_solution(8872837162201003742)
XLA Ops:
  0.0 0.7 pad_maximum_fusion
  0.7 0.1 broadcast_in_dim.8.scale
  0.8 1.6 %copy.10 = bf16[48,64,128]{2,0,1:T(8,128)(2,1)S(1)} copy(bf16[48,64,128]{2,1,0:T(8,128)(2,1)} %param.5) | data formatting | bytes 1572864 | tf_op args[0]
  2.5 0.0 copy-start
  2.5 0.0 copy-start.1
  2.5 1.9 %copy.7 = bf16[48,64,128]{1,0,2:T(8,128)(2,1)S(1)} copy(bf16[48,64,128]{2,1,0:T(8,128)(2,1)} %param.5) | data formatting | bytes 1572864 | tf_op args[0]
  4.4 0.0 copy-done
  4.4 0.0 copy-done.1
  4.5 79.4 %shard_map.55 = bf16[64,48,128]{2,1,0:T(8,128)(2,1)S(1)} custom-call(bf16[64,48,128]{2,1,0:T(8,128)(2,1)S(1)} %bitcast.9, bf16[128,48,64]{2,1,0:T(8,128)(2,1)S(1)} %bitcast.7, bf16[18,48,48]{2,1,0:T(8,128)(2,1)S(1)} %bitcast.10, bf16[2,48,48]{2,1,0:T(8,128)(2,1)S(1)} %copy-done.1, f32[8,48,128]{2,1,0:T(8,128)S(1)} %broadcast_in_dim.8.scale), custom_call_target="tpu_custom_call" | custom-call | flops 1358954496 | bytes 2359296 | tf_op jit(solution)/shard_map/pallas_call | solution.py:434
  83.8 1.1 %copy.8 = bf16[48,64,128]{2,1,0:T(8,128)(2,1)} copy(bf16[48,64,128]{2,0,1:T(8,128)(2,1)S(1)} %bitcast.8) | data formatting | bytes 1572864 | tf_op jit(solution)/shard_map/transpose | solution.py:469
Async XLA Ops:
  2.5 2.0 %copy-start = (bf16[2,3,3,48,48]{4,3,2,1,0:T(8,128)(2,1)S(1)}, bf16[2,3,3,48,48]{4,3,2,1,0:T(8,128)(2,1)}, u32[]{:S(2)}) copy-start(bf16[2,3,3,48,48]{4,3,2,1,0:T(8,128)(2,1)} %param.6) | copy-start | bytes 248836
  2.5 2.0 %copy-start.1 = (bf16[2,48,48]{2,1,0:T(8,128)(2,1)S(1)}, bf16[2,48,48]{2,1,0:T(8,128)(2,1)}, u32[]{:S(2)}) copy-start(bf16[2,48,48]{2,1,0:T(8,128)(2,1)} %w_point.1) | copy-start | bytes 27652

commit v4 on v3

--- a/solution.py
+++ b/solution.py
@@ -267,14 +267,15 @@
             pl.when(x["straight"])(x["straight_copy"].start)
             pl.when(x["stays"])(x["keep"].start)
 
-    def forward(self, piece):
-        for at, when, _, copy, arrival in self.through:
-            if at == piece:
-
-                @pl.when(when)
-                def _():
-                    arrival.wait_recv()
-                    copy.start()
+    def forward(self, piece, turn, turns):
+        passing = [x for x in self.through if x[0] == piece]
+        share = -(-len(passing) // turns)
+        for _, when, _, copy, arrival in passing[turn * share : (turn + 1) * share]:
+
+            @pl.when(when)
+            def _():
+                arrival.wait_recv()
+                copy.start()
 
     def arrive(self):
         for x in self.out:
@@ -289,9 +290,9 @@
 
 
 def kernel(
-    n_row, n_col, tile, turned, w_taps, w_point, scale, out,
+    n_row, n_col, tile, turned, w_taps, w_point, gain, bias, out,
     fx, tx, sx, fl, fr, tl, tr_, sl, sr, ff, flast, tf, tlast, sf, slast,
-    y0, parcel, mirror, relay, w_first, w_turned, w_second, lanes,
+    y0, parcel, mirror, relay, w_first, w_turned, w_second, lanes, scale,
     local, m_send, m_recv, l_send, l_recv, h_send, h_recv,
 ):
     r, c = lax.axis_index("row"), lax.axis_index("col")
@@ -319,6 +320,7 @@
     expected = swap.greet(barrier, expected)
 
     half = rows // ratio
+    groups = rows // PACK
 
     @pl.loop(0, half)
     def _(j):
@@ -326,38 +328,45 @@
             pair = [turned[h * rows + ratio * j + k] for k in range(ratio)]
             parcel[h, j] = jnp.concatenate(pair, axis=1)
 
+    own.wait()
+    pack_sides(fx, d0, ff, flast, groups, tc)
+    f_halo = halo(fx, fl, fr, ff, flast, d0, rows, n_row, n_col, h_send.at[0], h_recv.at[0])
     pl.semaphore_wait(barrier, expected)
 
+    start(f_halo)
     swap.start()
 
-    own.wait()
-    groups = rows // PACK
-    f_halo = halo(fx, fl, fr, ff, flast, d0, rows, n_row, n_col, h_send.at[0], h_recv.at[0])
-    start(f_halo[:2])
-    pack_sides(fx, d0, ff, flast, groups, tc)
-    start(f_halo[2:])
     t_halo = halo(tx, tl, tr_, tf, tlast, d0, rows, n_row, n_col, h_send.at[1], h_recv.at[1])
     s_halo = halo(sx, sl, sr, sf, slast, d1, rows, n_row, n_col, h_send.at[2], h_recv.at[2])
     clear(f_halo)
     clear(t_halo)
     clear(s_halo)
     fill_weights(w_taps, w_first, w_turned, w_second, ch)
-    swap.forward(1)
+    for layer in range(2):
+        for n in range(2):
+            for at, ref in ((0, gain), (2, bias)):
+                line = jnp.broadcast_to(ref[layer, n : n + 1, :], (tc, ch))
+                scale[4 * layer + at + n] = line.T
+    swap.forward(1, 0, 1)
     shift_rows(fx, lanes, d0, rows, d0, ch, tc)
     finish(f_halo)
     border_rows(fx, fl, fr, lanes, rows, d0, ch, tc)
     unroll = 4
-
-    @pl.loop(0, rows // unroll)
-    def _(t):
-        hidden = hidden_rows(lanes, w_first, t * unroll, unroll, d0, ch, tc, scale, 0)
-        branch = jnp.dot(w_point[0], hidden, preferred_element_type=F32)
-        for u in range(unroll):
-            row = t * unroll + u
-            y = branch[:, u * tc : (u + 1) * tc] * scale[1] + scale[3]
-            y0[row] = (fx[d0 + row].astype(F32) + y).astype(BF16)
-
-    swap.forward(0)
+    steps = rows // unroll
+    turns = 4
+    for turn in range(turns):
+
+        @pl.loop(turn * steps // turns, (turn + 1) * steps // turns)
+        def _(t):
+            hidden = hidden_rows(lanes, w_first, t * unroll, unroll, d0, ch, tc, scale, 0)
+            branch = jnp.dot(w_point[0], hidden, preferred_element_type=F32)
+            for u in range(unroll):
+                row = t * unroll + u
+                y = branch[:, u * tc : (u + 1) * tc] * scale[1] + scale[3]
+                y0[row] = (fx[d0 + row].astype(F32) + y).astype(BF16)
+
+        swap.forward(0, turn, turns)
+
     swap.arrive()
 
     @pl.loop(0, half)
@@ -420,8 +429,6 @@
     tile = jnp.transpose(features, (1, 0, 2))
     turned = jnp.transpose(features, (2, 0, 1))
     w_taps = w_dilated.reshape(-1, ch, ch)
-    scale = jnp.concatenate([norm_gain, norm_bias], axis=1).reshape(8, ch, 1)
-    scale = jnp.broadcast_to(scale, (8, ch, tc))
     d0, d1 = FIRST_DILATION, SECOND_DILATION
     groups = rows // PACK
 
@@ -434,8 +441,7 @@
     result = pl.pallas_call(
         functools.partial(kernel, n_row, n_col),
         out_shape=jax.ShapeDtypeStruct((rows, ch, tc), BF16),
-        in_specs=[pl.BlockSpec(memory_space=pl.ANY)]
-        + [pl.BlockSpec(memory_space=pltpu.VMEM)] * 4,
+        in_specs=[pl.BlockSpec(memory_space=pltpu.VMEM)] * 6,
         out_specs=pl.BlockSpec(memory_space=pltpu.VMEM),
         scratch_shapes=[
             vmem(rows + 2 * d0, ch, tc),
@@ -451,6 +457,7 @@
             vmem(ch, 9 * ch),
             vmem(2 * ch, 9 * ch),
             vmem(rows + 2 * d1, 3 * ch, tc),
+            vmem(8, ch, tc, dtype=F32),
             pltpu.SemaphoreType.DMA((3,)),
             pltpu.SemaphoreType.DMA((2, ratio)),
             pltpu.SemaphoreType.DMA((2, ratio)),
@@ -465,7 +472,7 @@
         cost_estimate=pl.CostEstimate(
             flops=4 * 2 * 9 * ch * ch * rows * tc, bytes_accessed=6 * ch * rows * tc, transcendentals=0
         ),
-    )(tile, turned, w_taps, w_pointwise, scale)
+    )(tile, turned, w_taps, w_pointwise, norm_gain, norm_bias)
     return jnp.transpose(result, (1, 0, 2))
 
 

time: 85.1 us -> 73.6 us (0.86)
  the two profiles are of different devices: /device:TPU:9 before, /device:TPU:11 now
where the time goes in v4:
time: 73.6 us; the launch traced here: 73.4 us
  Pallas kernels  69.5 us (94%)
  local copies, waits for them, and re-layouts  3.82 us (5%)
    pallas_call x1, Pallas kernels, body(): pl.pallas_call(functools.partial(kernel, n_row, n_col), out_shape=jax.Sha...  69.5 us
    unnamed x12, local copies, waits for them, and re-layouts  2.73 us

profile of v4, /device:TPU:11, one launch (start us, length us, event | category | flops | bytes accessed | tf_op | source)
XLA Modules:
  0.0 73.4 jit_solution(1025319836601705043)
XLA Ops:
  0.0 0.0 copy-start.4
  0.0 1.7 %copy.10 = bf16[48,64,128]{2,0,1:T(8,128)(2,1)S(1)} copy(bf16[48,64,128]{2,1,0:T(8,128)(2,1)} %param.5) | data formatting | bytes 1572864 | tf_op args[0]
  1.7 0.0 copy-start
  1.7 0.0 copy-start.1
  1.7 0.0 copy-start.2
  1.8 0.0 copy-start.3
  1.8 0.0 copy-done.4
  1.8 1.0 %copy.7 = bf16[48,64,128]{1,0,2:T(8,128)(2,1)S(1)} copy(bf16[48,64,128]{2,1,0:T(8,128)(2,1)S(1)} %copy-done.4) | data formatting | bytes 1572864 | tf_op args[0]
  2.8 0.0 copy-done
  2.8 0.0 copy-done.1
  2.8 0.0 copy-done.2
  2.8 0.0 copy-done.3
  2.8 69.5 %shard_map.55 = bf16[64,48,128]{2,1,0:T(8,128)(2,1)S(1)} custom-call(bf16[64,48,128]{2,1,0:T(8,128)(2,1)S(1)} %bitcast.8, bf16[128,48,64]{2,1,0:T(8,128)(2,1)S(1)} %bitcast.6, bf16[18,48,48]{2,1,0:T(8,128)(2,1)S(1)} %bitcast.9, bf16[2,48,48]{2,1,0:T(8,128)(2,1)S(1)} %copy-done.1, f32[2,2,48]{2,1,0:T(2,128)S(1)} %copy-done.2, f32[2,2,48]{2,1,0:T(2,128)S(1)} %copy-done.3), custom_call_target="tpu_custom_call" | custom-call | flops 1358954496 | bytes 2359296 | tf_op jit(solution)/shard_map/pallas_call | solution.py:441
  72.3 1.1 %copy.8 = bf16[48,64,128]{2,1,0:T(8,128)(2,1)} copy(bf16[48,64,128]{2,0,1:T(8,128)(2,1)S(1)} %bitcast.7) | data formatting | bytes 1572864 | tf_op jit(solution)/shard_map/transpose | solution.py:476
Async XLA Ops:
  0.0 1.8 %copy-start.4 = (bf16[48,64,128]{2,1,0:T(8,128)(2,1)S(1)}, bf16[48,64,128]{2,1,0:T(8,128)(2,1)}, u32[]{:S(2)}) copy-start(bf16[48,64,128]{2,1,0:T(8,128)(2,1)} %param.5) | copy-start | bytes 2359300
  1.7 1.1 %copy-start = (bf16[2,3,3,48,48]{4,3,2,1,0:T(8,128)(2,1)S(1)}, bf16[2,3,3,48,48]{4,3,2,1,0:T(8,128)(2,1)}, u32[]{:S(2)}) copy-start(bf16[2,3,3,48,48]{4,3,2,1,0:T(8,128)(2,1)} %param.6) | copy-start | bytes 248836
  1.7 1.1 %copy-start.1 = (bf16[2,48,48]{2,1,0:T(8,128)(2,1)S(1)}, bf16[2,48,48]{2,1,0:T(8,128)(2,1)}, u32[]{:S(2)}) copy-start(bf16[2,48,48]{2,1,0:T(8,128)(2,1)} %w_point.1) | copy-start | bytes 27652
  1.7 1.1 %copy-start.2 = (f32[2,2,48]{2,1,0:T(2,128)S(1)}, f32[2,2,48]{2,1,0:T(2,128)}, u32[]{:S(2)}) copy-start(f32[2,2,48]{2,1,0:T(2,128)} %gain.1) | copy-start | bytes 2308
  1.8 1.0 %copy-start.3 = (f32[2,2,48]{2,1,0:T(2,128)S(1)}, f32[2,2,48]{2,1,0:T(2,128)}, u32[]{:S(2)}) copy-start(f32[2,2,48]{2,1,0:T(2,128)} %bias.1) | copy-start | bytes 2308

commit v5 on v4

--- a/solution.py
+++ b/solution.py
@@ -95,8 +95,8 @@
             lanes[e, 2 * ch :] = jnp.concatenate([x[:, d:], x[:, :d]], axis=1)
 
 
-def patch_sides(left, right, lanes, groups, d, ch, tc):
-    @pl.loop(0, groups)
+def patch_sides(left, right, lanes, first, last, d, ch, tc):
+    @pl.loop(first, last)
     def _(g):
         lg = jnp.maximum(left[g], jnp.zeros((), BF16))
         rg = jnp.maximum(right[g], jnp.zeros((), BF16))
@@ -109,7 +109,14 @@
 def border_rows(main, left, right, lanes, rows, d, ch, tc):
     shift_rows(main, lanes, 0, d, d, ch, tc)
     shift_rows(main, lanes, rows + d, d, d, ch, tc)
-    patch_sides(left, right, lanes, (rows + 2 * d) // PACK, d, ch, tc)
+    hg, groups = d // PACK, rows // PACK
+    patch_sides(left, right, lanes, 0, hg, d, ch, tc)
+    patch_sides(left, right, lanes, hg + groups, 2 * hg + groups, d, ch, tc)
+
+
+def own_sides(left, right, lanes, rows, d, ch, tc):
+    first = d // PACK
+    patch_sides(left, right, lanes, first, first + rows // PACK, d, ch, tc)
 
 
 def hidden_rows(lanes, weights, row, count, d, ch, tc, scale, layer):
@@ -277,8 +284,8 @@
                 arrival.wait_recv()
                 copy.start()
 
-    def arrive(self):
-        for x in self.out:
+    def arrive(self, piece):
+        for x in self.out[piece * self.ratio : (piece + 1) * self.ratio]:
             pl.when(jnp.logical_not(x["stays"]))(x["arrival"].wait_recv)
             pl.when(x["stays"])(x["keep"].wait)
 
@@ -350,6 +357,7 @@
     swap.forward(1, 0, 1)
     shift_rows(fx, lanes, d0, rows, d0, ch, tc)
     finish(f_halo)
+    own_sides(fl, fr, lanes, rows, d0, ch, tc)
     border_rows(fx, fl, fr, lanes, rows, d0, ch, tc)
     unroll = 4
     steps = rows // unroll
@@ -367,52 +375,68 @@
 
         swap.forward(0, turn, turns)
 
-    swap.arrive()
-
-    @pl.loop(0, half)
-    def _(j):
-        pieces = [mirror[h, j] for h in range(ratio)]
-        for k in range(ratio):
-            tx[d0 + ratio * j + k] = jnp.concatenate(
-                [x[:, k * rows : (k + 1) * rows] for x in pieces], axis=1
-            )
-
-    start(t_halo[:2])
+    def unpack(first, last):
+        @pl.loop(first, last)
+        def _(j):
+            pieces = [mirror[h, j] for h in range(ratio)]
+            for k in range(ratio):
+                tx[d0 + ratio * j + k] = jnp.concatenate(
+                    [x[:, k * rows : (k + 1) * rows] for x in pieces], axis=1
+                )
+
+    swap.arrive(1)
+    unpack(swap.cut, half)
+    start(t_halo[:1])
+    swap.arrive(0)
+    unpack(0, swap.cut)
+    start(t_halo[1:2])
     pack_sides(tx, d0, tf, tlast, groups, tc)
     start(t_halo[2:])
     shift_rows(tx, lanes, d0, rows, d0, ch, tc)
     finish(t_halo)
+    own_sides(tl, tr_, lanes, rows, d0, ch, tc)
     border_rows(tx, tl, tr_, lanes, rows, d0, ch, tc)
 
-    @pl.loop(0, rows // unroll)
-    def _(t):
-        hidden = hidden_rows(lanes, w_turned, t * unroll, unroll, d0, ch, tc, scale, 0)
-        branch = jnp.dot(w_point[0], hidden, preferred_element_type=F32)
-        for u in range(unroll):
-            row = t * unroll + u
-            y = branch[:, u * tc : (u + 1) * tc] * scale[1] + scale[3]
-            y = (tx[d0 + row].astype(F32) + y).astype(BF16).astype(F32)
-            sx[d1 + row] = ((y + y0[row].astype(F32)) * 0.5).astype(BF16)
-
+    def first_block(first, last):
+        @pl.loop(first, last)
+        def _(t):
+            hidden = hidden_rows(lanes, w_turned, t * unroll, unroll, d0, ch, tc, scale, 0)
+            branch = jnp.dot(w_point[0], hidden, preferred_element_type=F32)
+            for u in range(unroll):
+                row = t * unroll + u
+                y = branch[:, u * tc : (u + 1) * tc] * scale[1] + scale[3]
+                y = (tx[d0 + row].astype(F32) + y).astype(BF16).astype(F32)
+                sx[d1 + row] = ((y + y0[row].astype(F32)) * 0.5).astype(BF16)
+
+    edge = d1 // unroll
+    first_block(0, edge)
+    first_block(steps - edge, steps)
     start(s_halo[:2])
+    first_block(edge, steps - edge)
     pack_sides(sx, d1, sf, slast, groups, tc)
     start(s_halo[2:])
     shift_rows(sx, lanes, d1, rows, d1, ch, tc)
-    finish(s_halo)
+    def second_block(first, last):
+        @pl.loop(first, last)
+        def _(t):
+            hidden = hidden_rows(lanes, w_second, t * unroll, unroll, d1, ch, tc, scale, 1)
+            branch = jnp.dot(w_point[1], hidden, preferred_element_type=F32)
+            for u in range(unroll):
+                row = t * unroll + u
+                x = sx[d1 + row].astype(F32)
+                both = []
+                for v in (u, u + unroll):
+                    y = branch[:, v * tc : (v + 1) * tc] * scale[5] + scale[7]
+                    both.append((x + y).astype(BF16).astype(F32))
+                out[row] = ((both[0] + both[1]) * 0.5).astype(BF16)
+
+    finish(s_halo[2:4])
+    own_sides(sl, sr, lanes, rows, d1, ch, tc)
+    second_block(edge, steps - edge)
+    finish(s_halo[:2] + s_halo[4:])
     border_rows(sx, sl, sr, lanes, rows, d1, ch, tc)
-
-    @pl.loop(0, rows // unroll)
-    def _(t):
-        hidden = hidden_rows(lanes, w_second, t * unroll, unroll, d1, ch, tc, scale, 1)
-        branch = jnp.dot(w_point[1], hidden, preferred_element_type=F32)
-        for u in range(unroll):
-            row = t * unroll + u
-            x = sx[d1 + row].astype(F32)
-            both = []
-            for v in (u, u + unroll):
-                y = branch[:, v * tc : (v + 1) * tc] * scale[5] + scale[7]
-                both.append((x + y).astype(BF16).astype(F32))
-            out[row] = ((both[0] + both[1]) * 0.5).astype(BF16)
+    second_block(0, edge)
+    second_block(steps - edge, steps)
 
     swap.finish()
     finish_sends(f_halo)

time: 73.6 us -> 65.2 us (0.89)
  Pallas kernels: 69.5 us -> 60.4 us
    pallas_call x1, Pallas kernels: 69.5 us -> 60.4 us  [body(): pl.pallas_call(functools.partial(kernel, n_row, n_col), out_shape=jax.Sha...]
where the time goes in v5:
time: 65.2 us; the launch traced here: 64.3 us
  Pallas kernels  60.4 us (93%)
  local copies, waits for them, and re-layouts  3.82 us (6%)
    pallas_call x1, Pallas kernels, body(): pl.pallas_call(functools.partial(kernel, n_row, n_col), out_shape=jax.Sha...  60.4 us
    unnamed x12, local copies, waits for them, and re-layouts  2.73 us

profile of v5, /device:TPU:11, one launch (start us, length us, event | category | flops | bytes accessed | tf_op | source)
XLA Modules:
  0.0 64.3 jit_solution(17966211668101091887)
XLA Ops:
  0.0 0.0 copy-start.4
  0.0 1.7 %copy.10 = bf16[48,64,128]{2,0,1:T(8,128)(2,1)S(1)} copy(bf16[48,64,128]{2,1,0:T(8,128)(2,1)} %param.5) | data formatting | bytes 1572864 | tf_op args[0]
  1.7 0.0 copy-start
  1.7 0.0 copy-start.1
  1.7 0.0 copy-start.2
  1.8 0.0 copy-start.3
  1.8 0.0 copy-done.4
  1.8 1.0 %copy.7 = bf16[48,64,128]{1,0,2:T(8,128)(2,1)S(1)} copy(bf16[48,64,128]{2,1,0:T(8,128)(2,1)S(1)} %copy-done.4) | data formatting | bytes 1572864 | tf_op args[0]
  2.8 0.0 copy-done
  2.8 0.0 copy-done.1
  2.8 0.0 copy-done.2
  2.8 0.0 copy-done.3
  2.8 60.4 %shard_map.55 = bf16[64,48,128]{2,1,0:T(8,128)(2,1)S(1)} custom-call(bf16[64,48,128]{2,1,0:T(8,128)(2,1)S(1)} %bitcast.8, bf16[128,48,64]{2,1,0:T(8,128)(2,1)S(1)} %bitcast.6, bf16[18,48,48]{2,1,0:T(8,128)(2,1)S(1)} %bitcast.9, bf16[2,48,48]{2,1,0:T(8,128)(2,1)S(1)} %copy-done.1, f32[2,2,48]{2,1,0:T(2,128)S(1)} %copy-done.2, f32[2,2,48]{2,1,0:T(2,128)S(1)} %copy-done.3), custom_call_target="tpu_custom_call" | custom-call | flops 1358954496 | bytes 2359296 | tf_op jit(solution)/shard_map/pallas_call | solution.py:465
  63.2 1.1 %copy.8 = bf16[48,64,128]{2,1,0:T(8,128)(2,1)} copy(bf16[48,64,128]{2,0,1:T(8,128)(2,1)S(1)} %bitcast.7) | data formatting | bytes 1572864 | tf_op jit(solution)/shard_map/transpose | solution.py:500
Async XLA Ops:
  0.0 1.8 %copy-start.4 = (bf16[48,64,128]{2,1,0:T(8,128)(2,1)S(1)}, bf16[48,64,128]{2,1,0:T(8,128)(2,1)}, u32[]{:S(2)}) copy-start(bf16[48,64,128]{2,1,0:T(8,128)(2,1)} %param.5) | copy-start | bytes 2359300
  1.7 1.1 %copy-start = (bf16[2,3,3,48,48]{4,3,2,1,0:T(8,128)(2,1)S(1)}, bf16[2,3,3,48,48]{4,3,2,1,0:T(8,128)(2,1)}, u32[]{:S(2)}) copy-start(bf16[2,3,3,48,48]{4,3,2,1,0:T(8,128)(2,1)} %param.6) | copy-start | bytes 248836
  1.7 1.1 %copy-start.1 = (bf16[2,48,48]{2,1,0:T(8,128)(2,1)S(1)}, bf16[2,48,48]{2,1,0:T(8,128)(2,1)}, u32[]{:S(2)}) copy-start(bf16[2,48,48]{2,1,0:T(8,128)(2,1)} %w_point.1) | copy-start | bytes 27652
  1.7 1.1 %copy-start.2 = (f32[2,2,48]{2,1,0:T(2,128)S(1)}, f32[2,2,48]{2,1,0:T(2,128)}, u32[]{:S(2)}) copy-start(f32[2,2,48]{2,1,0:T(2,128)} %gain.1) | copy-start | bytes 2308
  1.8 1.0 %copy-start.3 = (f32[2,2,48]{2,1,0:T(2,128)S(1)}, f32[2,2,48]{2,1,0:T(2,128)}, u32[]{:S(2)}) copy-start(f32[2,2,48]{2,1,0:T(2,128)} %bias.1) | copy-start | bytes 2308

commit v6 on v5

--- a/solution.py
+++ b/solution.py
@@ -22,8 +22,8 @@
     return (r >= 0) & (r < n_row) & (c >= 0) & (c < n_col)
 
 
-def pack_sides(main, offset, side_first, side_last, groups, tc):
-    @pl.loop(0, groups)
+def pack_sides(main, offset, side_first, side_last, first, last, tc):
+    @pl.loop(first, last)
     def _(g):
         rows = [main[offset + g * PACK + k] for k in range(PACK)]
         side_first[g] = jnp.concatenate([x[:, :SIDE] for x in rows], axis=1)
@@ -336,7 +336,7 @@
             parcel[h, j] = jnp.concatenate(pair, axis=1)
 
     own.wait()
-    pack_sides(fx, d0, ff, flast, groups, tc)
+    pack_sides(fx, d0, ff, flast, 0, groups, tc)
     f_halo = halo(fx, fl, fr, ff, flast, d0, rows, n_row, n_col, h_send.at[0], h_recv.at[0])
     pl.semaphore_wait(barrier, expected)
 
@@ -384,19 +384,6 @@
                     [x[:, k * rows : (k + 1) * rows] for x in pieces], axis=1
                 )
 
-    swap.arrive(1)
-    unpack(swap.cut, half)
-    start(t_halo[:1])
-    swap.arrive(0)
-    unpack(0, swap.cut)
-    start(t_halo[1:2])
-    pack_sides(tx, d0, tf, tlast, groups, tc)
-    start(t_halo[2:])
-    shift_rows(tx, lanes, d0, rows, d0, ch, tc)
-    finish(t_halo)
-    own_sides(tl, tr_, lanes, rows, d0, ch, tc)
-    border_rows(tx, tl, tr_, lanes, rows, d0, ch, tc)
-
     def first_block(first, last):
         @pl.loop(first, last)
         def _(t):
@@ -408,12 +395,31 @@
                 y = (tx[d0 + row].astype(F32) + y).astype(BF16).astype(F32)
                 sx[d1 + row] = ((y + y0[row].astype(F32)) * 0.5).astype(BF16)
 
-    edge = d1 // unroll
-    first_block(0, edge)
-    first_block(steps - edge, steps)
+    swap.arrive(1)
+    unpack(swap.cut, half)
+    start(t_halo[:1])
+    upper = groups // 2
+    pack_sides(tx, d0, tf, tlast, upper, groups, tc)
+    shift_rows(tx, lanes, d0 + upper * PACK, rows - upper * PACK, d0, ch, tc)
+    swap.arrive(0)
+    unpack(0, swap.cut)
+    start(t_halo[1:2])
+    pack_sides(tx, d0, tf, tlast, 0, upper, tc)
+    start(t_halo[2:])
+    shift_rows(tx, lanes, d0, upper * PACK, d0, ch, tc)
+    finish(t_halo[2:4])
+    own_sides(tl, tr_, lanes, rows, d0, ch, tc)
+    inner, edge = d0 // unroll, d1 // unroll
+    first_block(inner, edge)
+    first_block(steps - edge, steps - inner)
+    finish(t_halo[:2] + t_halo[4:])
+    border_rows(tx, tl, tr_, lanes, rows, d0, ch, tc)
+
+    first_block(0, inner)
+    first_block(steps - inner, steps)
     start(s_halo[:2])
     first_block(edge, steps - edge)
-    pack_sides(sx, d1, sf, slast, groups, tc)
+    pack_sides(sx, d1, sf, slast, 0, groups, tc)
     start(s_halo[2:])
     shift_rows(sx, lanes, d1, rows, d1, ch, tc)
     def second_block(first, last):

time: 65.2 us -> 65.3 us (level)
  the two profiles are of different devices: /device:TPU:11 before, /device:TPU:19 now
where the time goes in v6:
time: 65.3 us; the launch traced here: 65.2 us
  Pallas kernels  61.3 us (94%)
  local copies, waits for them, and re-layouts  3.82 us (6%)
    pallas_call x1, Pallas kernels, body(): pl.pallas_call(functools.partial(kernel, n_row, n_col), out_shape=jax.Sha...  61.3 us
    unnamed x12, local copies, waits for them, and re-layouts  2.73 us

profile of v6, /device:TPU:19, one launch (start us, length us, event | category | flops | bytes accessed | tf_op | source)
XLA Modules:
  0.0 65.2 jit_solution(7789459238464699569)
XLA Ops:
  0.0 0.0 copy-start.4
  0.0 1.7 %copy.10 = bf16[48,64,128]{2,0,1:T(8,128)(2,1)S(1)} copy(bf16[48,64,128]{2,1,0:T(8,128)(2,1)} %param.5) | data formatting | bytes 1572864 | tf_op args[0]
  1.7 0.0 copy-start
  1.7 0.0 copy-start.1
  1.7 0.0 copy-start.2
  1.8 0.0 copy-start.3
  1.8 0.0 copy-done.4
  1.8 1.0 %copy.7 = bf16[48,64,128]{1,0,2:T(8,128)(2,1)S(1)} copy(bf16[48,64,128]{2,1,0:T(8,128)(2,1)S(1)} %copy-done.4) | data formatting | bytes 1572864 | tf_op args[0]
  2.8 0.0 copy-done
  2.8 0.0 copy-done.1
  2.8 0.0 copy-done.2
  2.8 0.0 copy-done.3
  2.8 61.3 %shard_map.55 = bf16[64,48,128]{2,1,0:T(8,128)(2,1)S(1)} custom-call(bf16[64,48,128]{2,1,0:T(8,128)(2,1)S(1)} %bitcast.8, bf16[128,48,64]{2,1,0:T(8,128)(2,1)S(1)} %bitcast.6, bf16[18,48,48]{2,1,0:T(8,128)(2,1)S(1)} %bitcast.9, bf16[2,48,48]{2,1,0:T(8,128)(2,1)S(1)} %copy-done.1, f32[2,2,48]{2,1,0:T(2,128)S(1)} %copy-done.2, f32[2,2,48]{2,1,0:T(2,128)S(1)} %copy-done.3), custom_call_target="tpu_custom_call" | custom-call | flops 1358954496 | bytes 2359296 | tf_op jit(solution)/shard_map/pallas_call | solution.py:471
  64.1 1.1 %copy.8 = bf16[48,64,128]{2,1,0:T(8,128)(2,1)} copy(bf16[48,64,128]{2,0,1:T(8,128)(2,1)S(1)} %bitcast.7) | data formatting | bytes 1572864 | tf_op jit(solution)/shard_map/transpose | solution.py:506
Async XLA Ops:
  0.0 1.8 %copy-start.4 = (bf16[48,64,128]{2,1,0:T(8,128)(2,1)S(1)}, bf16[48,64,128]{2,1,0:T(8,128)(2,1)}, u32[]{:S(2)}) copy-start(bf16[48,64,128]{2,1,0:T(8,128)(2,1)} %param.5) | copy-start | bytes 2359300
  1.7 1.1 %copy-start = (bf16[2,3,3,48,48]{4,3,2,1,0:T(8,128)(2,1)S(1)}, bf16[2,3,3,48,48]{4,3,2,1,0:T(8,128)(2,1)}, u32[]{:S(2)}) copy-start(bf16[2,3,3,48,48]{4,3,2,1,0:T(8,128)(2,1)} %param.6) | copy-start | bytes 248836
  1.7 1.1 %copy-start.1 = (bf16[2,48,48]{2,1,0:T(8,128)(2,1)S(1)}, bf16[2,48,48]{2,1,0:T(8,128)(2,1)}, u32[]{:S(2)}) copy-start(bf16[2,48,48]{2,1,0:T(8,128)(2,1)} %w_point.1) | copy-start | bytes 27652
  1.7 1.1 %copy-start.2 = (f32[2,2,48]{2,1,0:T(2,128)S(1)}, f32[2,2,48]{2,1,0:T(2,128)}, u32[]{:S(2)}) copy-start(f32[2,2,48]{2,1,0:T(2,128)} %gain.1) | copy-start | bytes 2308
  1.8 1.0 %copy-start.3 = (f32[2,2,48]{2,1,0:T(2,128)S(1)}, f32[2,2,48]{2,1,0:T(2,128)}, u32[]{:S(2)}) copy-start(f32[2,2,48]{2,1,0:T(2,128)} %bias.1) | copy-start | bytes 2308
